TPU v7x, 128 devices: a whole 4x4x4 slice. The times are simulated.
128 devices in a mesh: ctx: 2 (over core), sess: 64 (over z, y, x).
Axes of the slice: x: 4, y: 4, z: 4, core: 2. Of those that a mesh axis runs over, the one named last changes fastest.
Arguments:
- query_rows: bfloat16 [64, 1536, 4096], P('sess', 'ctx'), may hold values from -6 to 6
- key_rows: bfloat16 [64, 1536, 4096], P('sess', 'ctx'), may hold values from -0.59765625 to 0.59765625
- value_rows: bfloat16 [64, 1536, 4096], P('sess', 'ctx'), may hold values from -6 to 6
- decay_rates: float32 [64, 1536, 32], P('sess', 'ctx'), may hold values from 0 to 1, as said below
- valid_blocks: int32 [64], P('sess'), may hold values from 1 to 6, as said below
- step_queries: bfloat16 [2048, 4, 4096], P('sess', None, 'ctx'), may hold values from -6 to 6
- step_keys: bfloat16 [2048, 4, 4096], P('sess', None, 'ctx'), may hold values from -3 to 3
- step_values: bfloat16 [2048, 4, 4096], P('sess', None, 'ctx'), may hold values from -6 to 6
- step_rates: bfloat16 [2048, 4, 32], P('sess', None, 'ctx'), may hold values from 0.019897461 to 0.69921875
- row_session: int32 [2048, 1], P('sess'), may hold values from 0 to 63; in each aligned block of 32 rows (0 to 31, 32 to 63, ...) no two rows name the same one
Outputs:
- prefill_out: bfloat16 [64, 1536, 4096], P('sess', 'ctx')
- decode_out: bfloat16 [2048, 4, 4096], P('sess', None, 'ctx')
Inputs may be any that keep to these rules, and one draw needn't show every extreme that they name: The blocks of 256 positions after the first valid_blocks of a session are padding; some session uses all 6. `decay_rates`: decay rates of the heads, positive. `row_session`: among the rows of one index of sess (aligned blocks of 32 rows) no session is named by more than 1 row, a bound that some block reaches; every session is named by some row.
All inputs are finite; a program needn't handle non-finite values.
Results may differ from a plain program's by a relative error of at most 0.0053.
Values may be sent and summed in bfloat16 or wider, within the bound.
A program may use at most 256 MiB of HBM per device.

v0:
```python
import jax
import jax.numpy as jnp
from jax import lax
from jax.sharding import PartitionSpec as P

BLK = 256


EPSILON = 1e-06


def prefix(value, axis, join, neutral):
    count, mine = (lax.axis_size(axis), lax.axis_index(axis))
    pieces = jax.tree.map(lambda part: lax.all_gather(part, axis), value)
    total = jax.tree.map(
        lambda part, zero: jnp.full_like(part, 0) + jnp.asarray(zero, part.dtype), value, neutral
    )

    def lap(position, total):
        longer = join(total, jax.tree.map(lambda part: part[position], pieces))
        return jax.tree.map(lambda new, old: jnp.where(position < mine, new, old), longer, total)

    return lax.fori_loop(0, count - 1, lap, total)


def from_root(value, axis, source):
    kept = jnp.where(lax.axis_index(axis) == source, value, 0).astype(value.dtype)
    return lax.psum(kept, axis)


def head_norm(values):
    return values * lax.rsqrt(jnp.mean(values * values, axis=-1, keepdims=True) + EPSILON)


def block_terms(queries, keys_part, values_part, rates_part):
    length = queries.shape[0]
    running_decay = jnp.cumsum(rates_part, axis=0)
    block_decay = running_decay[-1]
    scores = jnp.einsum("thd,shd->hts", queries, keys_part, preferred_element_type=jnp.float32)
    decay_gap = running_decay.T[:, :, None] - running_decay.T[:, None, :]
    causal_mask = jnp.arange(length)[:, None] >= jnp.arange(length)[None, :]
    weights = jnp.where(causal_mask, jnp.exp(-jnp.where(causal_mask, decay_gap, 0.0)), 0.0)
    mixed_scores = (scores * weights).astype(jnp.bfloat16)
    within = jnp.einsum(
        "hts,shd->thd", mixed_scores, values_part, preferred_element_type=jnp.float32
    )
    weighted = (
        keys_part.astype(jnp.float32) * jnp.exp(running_decay - block_decay)[:, :, None]
    ).astype(jnp.bfloat16)
    increment = jnp.einsum(
        "shd,she->hde", weighted, values_part, preferred_element_type=jnp.float32
    )
    return (running_decay, block_decay, within, increment)


def chain_combine(earlier, latter):
    return (earlier[0] + latter[0], jnp.exp(-latter[0])[:, None, None] * earlier[1] + latter[1])


def decode_rows(projected, queries, keys_part, values_part, rates_part):
    steps_count = queries.shape[1]
    log_factor = jnp.cumsum(-rates_part.astype(jnp.float32), axis=1)
    queries_wide = queries.astype(jnp.float32)
    keys_wide = keys_part.astype(jnp.float32)
    values_wide = values_part.astype(jnp.float32)
    affinity = jnp.einsum(
        "nihd,njhd->nhij", queries_wide, keys_wide, precision=lax.Precision.HIGHEST
    )
    gap = (
        log_factor.transpose(0, 2, 1)[:, :, :, None] - log_factor.transpose(0, 2, 1)[:, :, None, :]
    )
    lower = jnp.arange(steps_count)[:, None] >= jnp.arange(steps_count)[None, :]
    decayed = jnp.where(lower, affinity * jnp.exp(jnp.where(lower, gap, 0.0)), 0.0)
    recent = jnp.einsum("nhij,njhe->nihe", decayed, values_wide, precision=lax.Precision.HIGHEST)
    reading = jnp.exp(log_factor)[:, :, :, None] * projected + recent
    return head_norm(reading).astype(jnp.bfloat16)


def local(
    query_rows,
    key_rows,
    value_rows,
    decay_rates,
    valid_blocks,
    step_queries,
    step_keys,
    step_values,
    step_rates,
    row_session,
):
    token_count = query_rows.shape[1]
    head_count = decay_rates.shape[2]
    head_width = query_rows.shape[2] // head_count
    first_position = lax.axis_index("ctx") * token_count
    positions = first_position + jnp.arange(token_count, dtype=jnp.int32)
    live_mask = positions < valid_blocks[0] * BLK
    live_rates = jnp.where(live_mask[:, None], decay_rates[0], 0.0)
    head_queries = query_rows[0].reshape(token_count, head_count, head_width)
    masked_keys = jnp.where(live_mask[:, None], key_rows[0], jnp.zeros_like(key_rows[0])).reshape(
        token_count, head_count, head_width
    )
    head_values = value_rows[0].reshape(token_count, head_count, head_width)
    block_parts = []
    local_state = jnp.zeros((head_count, head_width, head_width), jnp.float32)
    device_decay = jnp.zeros((head_count,), jnp.float32)
    for block_index in range(token_count // BLK):
        window = slice(block_index * BLK, (block_index + 1) * BLK)
        block_queries = head_queries[window]
        running_decay, block_decay, within, increment = block_terms(
            block_queries, masked_keys[window], head_values[window], live_rates[window]
        )
        block_parts.append((block_queries, running_decay, within, local_state, device_decay))
        local_state = jnp.exp(-block_decay)[:, None, None] * local_state + increment
        device_decay = device_decay + block_decay
    prefix_decay, prefix_state = prefix(
        (device_decay, local_state),
        "ctx",
        chain_combine,
        (jnp.zeros_like(device_decay), jnp.zeros_like(local_state)),
    )
    normed_blocks = []
    for block_queries, running_decay, within, entering_local, decay_before in block_parts:
        entering = (jnp.exp(-decay_before)[:, None, None] * prefix_state + entering_local).astype(
            jnp.bfloat16
        )
        across = jnp.exp(-running_decay)[:, :, None] * jnp.einsum(
            "thd,hde->the", block_queries, entering, preferred_element_type=jnp.float32
        )
        normed_blocks.append(head_norm(within + across))
    normed = jnp.concatenate(normed_blocks, axis=0) * live_mask[:, None, None]
    prefill_out = normed.astype(jnp.bfloat16).reshape(1, token_count, head_count * head_width)
    head_share = head_count // lax.axis_size("ctx")
    inclusive = jnp.exp(-device_decay)[:, None, None] * prefix_state + local_state
    whole_state = from_root(inclusive, "ctx", lax.axis_size("ctx") - 1)
    session_heads = lax.dynamic_slice_in_dim(
        whole_state, lax.axis_index("ctx") * head_share, head_share, 0
    )
    row_count = step_queries.shape[0]
    steps_count = step_queries.shape[1]
    share_width = step_queries.shape[2]

    def split_heads(data):
        return data.reshape(data.shape[0], steps_count, head_share, head_width)

    every_session = lax.all_gather(session_heads[None], "sess", axis=0, tiled=True)
    split_queries = split_heads(step_queries)

    def project_row(item):
        session_id, row_queries = item
        picked = lax.dynamic_index_in_dim(every_session, session_id, 0, keepdims=False)
        return jnp.einsum(
            "shd,hde->she", row_queries.astype(jnp.float32), picked, precision=lax.Precision.HIGHEST
        )

    projected = lax.map(project_row, (row_session[:, 0], split_queries))
    decoded = decode_rows(
        projected, split_queries, split_heads(step_keys), split_heads(step_values), step_rates
    )
    decode_out = decoded.reshape(row_count, steps_count, share_width)
    return (prefill_out, decode_out)


def solution(mesh):
    placed = (
        P("sess", "ctx", None),
        P("sess", "ctx", None),
        P("sess", "ctx", None),
        P("sess", "ctx", None),
        P("sess"),
        P("sess", None, "ctx"),
        P("sess", None, "ctx"),
        P("sess", None, "ctx"),
        P("sess", None, "ctx"),
        P("sess", None),
    )
    return jax.shard_map(
        local,
        mesh=mesh,
        in_specs=placed,
        out_specs=(P("sess", "ctx", None), P("sess", None, "ctx")),
        check_vma=False,
    )
```

profile of v0, /device:TPU:1, one launch (start us, length us, event | category | flops | bytes accessed | tf_op | source)
XLA Modules:
  0.0 555.2 jit_solution(3361917049239338968)
XLA Ops:
  12.1 5.5 fusion.72
  17.6 4.1 copy.237
  21.7 8.6 %copy.231 = bf16[1,768,4096]{1,2,0:T(8,128)(2,1)} copy(bf16[1,768,4096]{2,1,0:T(8,128)(2,1)} %param.13) | data formatting | bytes 12582912 | tf_op args[1]
  36.4 4.1 copy.291
  54.4 17.2 %all-gather.6.cloned.1.call-done = f32[64,128,128]{2,1,0:T(8,128)} async-done(((f32[32,128,128]{2,1,0:T(8,128)}), f32[64,128,128]{2,1,0:T(8,128)}) %all-gather.6.cloned.1.call-update) | async-done | bytes 4194320 | tf_op jit(solution)/shard_map/all_gather | solution.py:14
  71.6 4.0 add_select_fusion
  75.7 28.2 %all-reduce.2.cloned.1.call-done = f32[32,128,128]{2,1,0:T(8,128)} async-done(((f32[32,128,128]{2,1,0:T(8,128)}), f32[32,128,128]{2,1,0:T(8,128)}) %all-reduce.2.cloned.1.call-update) | async-done | bytes 2097168 | tf_op jit(solution)/shard_map/psum | solution.py:28
  106.3 5.8 %fusion.70 = (bf16[1,256,4096]{2,1,0:T(8,128)(2,1)}, bf16[1,256,4096]{2,1,0:T(8,128)(2,1)}, bf16[1,256,4096]{2,1,0:T(8,128)(2,1)}) fusion(bf16[1,768,4096]{2,1,0:T(8,128)(2,1)} %param.12), kind=kLoop, calls=%fused_computation.130 | loop fusion | bytes 12582912 | tf_op jit(solution)/shard_map/slice | solution.py:108
  112.0 4.1 copy.294
  116.1 4.1 copy.293
  120.2 4.3 copy.290
  128.1 8.2 %fusion.14 = f32[32,256,128]{1,2,0:T(8,128)} fusion(bf16[256,32,128]{0,2,1:T(8,128)(2,1)} %bitcast.187, f32[32,256]{1,0:T(8,128)S(1)} %get-tuple-element.85, pred[256,256]{0,1:T(8,128)(4,1)S(1)} %iota_compare_fusion, bf16[256,32,128]{0,2,1:T(8,128)(2,1)} %bitcast.193, bf16[256,32,128]{0,2,1:T(8,128)(2,1)} %bitcast.191), kind=kOutput, calls=%fused_computation.18 | convolution fusion | flops 1086324736 | bytes 10584064 | tf_op jit(solution)/shard_map/hts,shd->thd/dot_general | solution.py:44
  136.3 8.0 %fusion.12 = f32[32,256,128]{1,2,0:T(8,128)} fusion(bf16[256,32,128]{0,2,1:T(8,128)(2,1)} %bitcast.179, f32[32,256]{1,0:T(8,128)S(1)} %get-tuple-element.80, pred[256,256]{0,1:T(8,128)(4,1)S(1)} %iota_compare_fusion, bf16[256,32,128]{0,2,1:T(8,128)(2,1)} %bitcast.185, bf16[256,32,128]{0,2,1:T(8,128)(2,1)} %bitcast.189), kind=kOutput, calls=%fused_computation.17 | convolution fusion | flops 1086324736 | bytes 10584064 | tf_op jit(solution)/shard_map/hts,shd->thd/dot_general | solution.py:44
  144.3 8.9 %fusion.10 = f32[32,256,128]{1,2,0:T(8,128)} fusion(bf16[256,32,128]{0,2,1:T(8,128)(2,1)} %bitcast.178, f32[32,256]{1,0:T(8,128)S(1)} %get-tuple-element.76, pred[256,256]{0,1:T(8,128)(4,1)S(1)} %iota_compare_fusion, bf16[256,32,128]{0,2,1:T(8,128)(2,1)} %bitcast.184, bf16[256,32,128]{0,2,1:T(8,128)(2,1)} %bitcast.181), kind=kOutput, calls=%fused_computation.16 | convolution fusion | flops 1086324736 | bytes 10584064 | tf_op jit(solution)/shard_map/hts,shd->thd/dot_general | solution.py:44
  153.2 5.5 multiply_reduce_fusion
  161.2 5.7 %copy.264 = f32[1,256,4096]{2,1,0:T(8,128)} copy(f32[1,256,4096]{1,2,0:T(8,128)} %bitcast.174) | data formatting | bytes 8388608 | tf_op jit(solution)/shard_map/concatenate | solution.py:130
  166.9 5.0 multiply_reduce_fusion.1
  174.3 5.9 %copy.263 = f32[1,256,4096]{2,1,0:T(8,128)} copy(f32[1,256,4096]{1,2,0:T(8,128)} %bitcast.175) | data formatting | bytes 8388608 | tf_op jit(solution)/shard_map/concatenate | solution.py:130
  180.2 3.9 multiply_reduce_fusion.2
  186.8 5.6 %copy.262 = f32[1,256,4096]{2,1,0:T(8,128)} copy(f32[1,256,4096]{1,2,0:T(8,128)} %bitcast.176) | data formatting | bytes 8388608 | tf_op jit(solution)/shard_map/concatenate | solution.py:130
  192.4 8.0 %fusion.6 = bf16[1,768,4096]{2,1,0:T(8,128)(2,1)} fusion(f32[1,256,4096]{2,1,0:T(8,128)} %copy.264, f32[1,256,4096]{2,1,0:T(8,128)} %copy.263, f32[1,256,4096]{2,1,0:T(8,128)} %copy.262, f32[768]{0:T(1024)S(1)} %fusion.63), kind=kLoop, calls=%fused_computation.8 | loop fusion | flops 12582912 | bytes 18877440 | tf_op jit(solution)/shard_map/convert_element_type | solution.py:131
  200.4 184.3 %all-gather.8.cloned.1.call-done = f32[1024,128,128]{2,1,0:T(8,128)} async-done(((f32[16,128,128]{2,1,0:T(8,128)}), f32[1024,128,128]{2,1,0:T(8,128)}) %all-gather.8.cloned.1.call-update) | async-done | bytes 67108880 | tf_op jit(solution)/shard_map/all_gather | solution.py:145
  384.7 158.4 %while.2 = (s32[]{:T(128)}, f32[32,4,16,128]{3,1,2,0:T(4,128)}, s32[32]{0:T(128)S(1)}, f32[64,16,128,128]{3,2,1,0:T(8,128)}, bf16[32,4,16,128]{3,1,2,0:T(4,128)(2,1)}, /*index=5*/s32[]{:T(128)}, s32[]{:T(128)}, s32[]{:T(128)}) while((s32[]{:T(128)}, f32[32,4,16,128]{3,1,2,0:T(4,128)}, s32[32]{0:T(128)S(1)}, ...), condition=%wide.region_12.13_spmd, body=%wide.region_11.12_spmd.sunk | while | flops 12582917 | bytes 1099403 | solution.py:155
  543.1 3.7 multiply_reduce_fusion.3
  (140 shorter events, 135.5 us)
Async XLA Ops:
  7.2 536.0 %copy-start = (bf16[32,4,2048]{2,1,0:T(4,128)(2,1)S(1)}, bf16[32,4,2048]{2,1,0:T(4,128)(2,1)}, u32[]{:S(2)}) copy-start(bf16[32,4,2048]{2,1,0:T(4,128)(2,1)} %param.19) | copy-start | bytes 1572868
  7.2 64.5 %all-gather.6.cloned.1.call-start = ((), (), s32[]{:S(2)}) async-start(), calls=%async_computation.1 | async-start | bytes 6291456 | tf_op jit(solution)/shard_map/all_gather | solution.py:14
  42.9 3.1 copy-start.2
  42.9 3.5 copy-start.4
  46.4 2.1 copy-start.5
  46.4 3.0 copy-start.6
  47.2 1.3 copy-start.1
  51.5 52.5 %all-reduce.2.cloned.1.call-start = ((), (), s32[]{:S(2)}) async-start(), calls=%async_computation | async-start | bytes 4194304 | tf_op jit(solution)/shard_map/psum | solution.py:28
  75.6 309.1 %all-gather.8.cloned.1.call-start = ((), (), s32[]{:S(2)}) async-start(), calls=%async_computation.2 | async-start | bytes 68157440 | tf_op jit(solution)/shard_map/all_gather | solution.py:145
  120.2 4.3 copy-start.7
  174.3 5.9 %copy-start.3 = (bf16[1,256,4096]{1,2,0:T(8,128)(2,1)S(1)}, bf16[1,256,4096]{1,2,0:T(8,128)(2,1)}, u32[]{:S(2)}) copy-start(bf16[1,256,4096]{1,2,0:T(8,128)(2,1)} %copy.290) | copy-start | bytes 6291460
  192.4 192.3 %copy-start.8 = (s32[32,1]{0,1:T(1,128)S(1)}, s32[32,1]{0,1:T(1,128)}, u32[]{:S(2)}) copy-start(s32[32,1]{0,1:T(1,128)} %param.21) | copy-start | bytes 388
Sparse Core Ops, SparseCore 0:
  51.6 20.0 all-gather.5
  75.8 28.1 all-reduce.1
  107.2 277.4 all-gather.7
where the time goes:
time: 558 us; the launch traced here: 555 us
  waiting for transfers between devices  230 us (41%)
  matrix products  130 us (23%)
  local copies, waits for them, and re-layouts  88.1 us (16%)
  loops' own time  62.2 us (11%)
  other arithmetic  27.7 us (5%)
  between operations  14.7 us (3%)
    all_gather x1, waiting for transfers between devices, local(): lax.all_gather(session_heads[None], 'sess', axis=0, tiled=True)  184 us
    dot_general x32, matrix products, project_row(): jnp.einsum('shd,hde->she', row_queries.astype(jnp.float32), picked, preci...  77.5 us
    another operation x1, loops' own time, local(): projected = lax.map(project_row, (row_session[:, 0], split_queries))  62.2 us
    unnamed x25, local copies, waits for them, and re-layouts  30.3 us
    psum x1, waiting for transfers between devices, from_root(): return lax.psum(kept, axis)  28.2 us
    dot_general x3, matrix products, block_terms(): jnp.einsum('hts,shd->thd', mixed_scores, values_part, preferred_element_t...  25.1 us
    dynamic_slice x32, local copies, waits for them, and re-layouts, local(): projected = lax.map(project_row, (row_session[:, 0], split_queries))  18.6 us
    concatenate x3, local copies, waits for them, and re-layouts, local(): normed = jnp.concatenate(normed_blocks, axis=0) * live_mask[:, None, None]  17.3 us
  transfers between devices with their start and end apart: 3, of which 3 were waited for; matrix products, arithmetic and copies ran while one was open for 17% of the time, Pallas kernels for 0%

commit v1 on v0

v1 whole, which is shorter than its diff:
```python
import functools

import jax
import jax.numpy as jnp
from jax import lax
from jax.experimental import pallas as pl
from jax.experimental.pallas import tpu as pltpu
from jax.sharding import PartitionSpec as P

BLK = 256
DH = 128
EPSILON = 1e-06
F32 = jnp.float32
BF16 = jnp.bfloat16
HIGH = lax.Precision.HIGHEST


def dot(a, b, dims=((1,), (0,)), precision=None):
    return lax.dot_general(a, b, (dims, ((), ())), precision=precision, preferred_element_type=F32)


def iota(shape, axis):
    return lax.broadcasted_iota(jnp.int32, shape, axis)


def prepare(rates, live, heads):
    lanes = iota((heads, 128), 1)
    copies = (lax.rem(lanes, heads) == iota((heads, 128), 0)).astype(F32)
    lower = (iota((BLK, BLK), 0) >= iota((BLK, BLK), 1)).astype(F32)
    wide = dot(rates * live, copies, precision=HIGH)
    running = dot(lower, wide, precision=HIGH)
    first = running.astype(BF16).astype(F32)
    second = (running - first).astype(BF16).astype(F32)
    third = running - first - second
    group = lax.div(iota((BLK, 128), 1), heads)
    parts = jnp.where(group == 0, first, jnp.where(group == 1, second, jnp.where(group == 2, third, 0.0)))
    return parts.astype(BF16), running.T


def spread_matrix(pair, heads):
    row, lane = iota((128, 2 * DH), 0), iota((128, 2 * DH), 1)
    wanted = pair * 2 + lax.div(lane, DH)
    return ((lax.rem(row, heads) == wanted) & (row < 3 * heads)).astype(F32).astype(BF16)


def live_factor(valid_ref, j, blocks):
    return (lax.axis_index("ctx") * blocks + j < valid_ref[0]).astype(F32)


def states_kernel(heads, blocks, valid_ref, rates_ref, k_ref, v_ref, mid_ref, end_ref, parts_scr):
    pair = pl.program_id(0)

    @pl.when(pair == 0)
    def _():
        for j in range(blocks):
            live = live_factor(valid_ref, j, blocks)
            parts_scr[j], _ = prepare(rates_ref[j * BLK:(j + 1) * BLK, :], live, heads)

    spread = spread_matrix(pair, heads)
    states = [jnp.zeros((DH, DH), F32)] * 2
    total = jnp.zeros((1, 2 * DH), F32)
    for j in range(blocks):
        rows = slice(j * BLK, (j + 1) * BLK)
        live = live_factor(valid_ref, j, blocks)
        running = dot(parts_scr[j], spread)
        last = running[BLK - 1:BLK, :]
        weighted = (k_ref[rows, :].astype(F32) * (jnp.exp(running - last) * live)).astype(BF16)
        decay = jnp.exp(-last)
        total = total + last
        for one in range(2):
            cols = slice(one * DH, (one + 1) * DH)
            if j > 0:
                mid_ref[one, j - 1] = states[one]
            states[one] = decay[:, cols] * states[one] + dot(weighted[:, cols], v_ref[rows, cols], ((0,), (0,)))
    for one in range(2):
        cols = slice(one * DH, (one + 1) * DH)
        end_ref[one, 0:DH, :] = states[one]
        end_ref[one, DH:DH + 8, :] = jnp.broadcast_to(jnp.exp(-total[:, cols]), (8, DH))


def outputs_kernel(heads, blocks, valid_ref, rates_ref, q_ref, k_ref, v_ref, mid_ref, prefix_ref, out_ref, parts_scr, turned_scr):
    pair = pl.program_id(0)

    @pl.when(pair == 0)
    def _():
        for j in range(blocks):
            live = live_factor(valid_ref, j, blocks)
            parts_scr[j], turned = prepare(rates_ref[j * BLK:(j + 1) * BLK, :], live, heads)
            turned_scr[j] = turned[0:heads, :]

    spread = spread_matrix(pair, heads)
    half = BLK // 2
    lower = iota((half, half), 0) >= iota((half, half), 1)
    before = jnp.zeros((1, 2 * DH), F32)
    for j in range(blocks):
        live = live_factor(valid_ref, j, blocks)
        running = dot(parts_scr[j], spread)
        from_start = jnp.exp(-running)
        for one in range(2):
            cols = slice(one * DH, (one + 1) * DH)
            row = turned_scr[j, pl.ds(pair * 2 + one, 1), :]
            run = running[:, cols]
            rows = slice(j * BLK, (j + 1) * BLK)
            q, k, v = q_ref[rows, cols], k_ref[rows, cols], v_ref[rows, cols]
            top, bottom = q[:half], q[half:]
            scores0 = dot(top, k[:half], ((1,), (1,)))
            scores1 = dot(bottom, k, ((1,), (1,)))
            mixed0 = jnp.where(lower, scores0 * jnp.exp(row[:, :half] - run[:half]), 0.0).astype(BF16)
            mixed10 = scores1[:, :half] * jnp.exp(row[:, :half] - run[half:])
            mixed11 = jnp.where(lower, scores1[:, half:] * jnp.exp(row[:, half:] - run[half:]), 0.0)
            mixed1 = jnp.concatenate([mixed10, mixed11], axis=1).astype(BF16)
            within = jnp.concatenate([dot(mixed0, v[:half]), dot(mixed1, v)], axis=0)
            entering = jnp.exp(-before[:, cols]) * prefix_ref[one, 0:DH, :]
            if j > 0:
                entering = entering + mid_ref[one, j - 1]
            mix = within + from_start[:, cols] * dot(q, entering.astype(BF16))
            scale = lax.rsqrt(jnp.mean(mix * mix, axis=1, keepdims=True) + EPSILON) * live
            out_ref[rows, cols] = (mix * scale).astype(BF16)
        before = before + running[BLK - 1:BLK, :]


def project_kernel(x_ref, mine_ref, other_ref, y_ref):
    quad = pl.program_id(0)
    first_core = lax.axis_index("ctx") == 0
    groups = x_ref.shape[0]
    x = x_ref[...].reshape(groups * 16, DH)
    doubled = jnp.concatenate([x, x], axis=1)
    position = lax.div(lax.rem(iota((groups * 16, DH), 0), 16), 4)
    chosen = None
    for two in range(2):
        columns = []
        for one in range(2):
            h = two * 2 + one
            earlier = jnp.where(first_core, mine_ref[h, 0:DH, :], other_ref[h, 0:DH, :])
            latter = jnp.where(first_core, other_ref[h, 0:DH, :], mine_ref[h, 0:DH, :])
            decay = jnp.where(first_core, other_ref[h, DH:DH + 1, :], mine_ref[h, DH:DH + 1, :])
            final = decay * earlier + latter
            upper = final.astype(BF16)
            rest = (final - upper.astype(F32)).astype(BF16)
            columns.append(jnp.concatenate([upper, rest], axis=0))
        product = dot(doubled, jnp.concatenate(columns, axis=1))
        for one in range(2):
            part = product[:, one * DH:(one + 1) * DH]
            chosen = part if chosen is None else jnp.where(position == two * 2 + one, part, chosen)
    y_ref[...] = chosen.astype(BF16).reshape(groups, 16, DH)


def shift_down(value, amount):
    return pltpu.roll(value, amount, 0)


def decode_kernel(q_ref, k_ref, v_ref, p_ref, g_ref, out_ref):
    q, k, v, p = (ref[...].astype(F32) for ref in (q_ref, k_ref, v_ref, p_ref))
    g = g_ref[...]
    reading = g[:, 4:5] * p
    for delta in range(4):
        kd = k if delta == 0 else shift_down(k, delta)
        vd = v if delta == 0 else shift_down(v, delta)
        affinity = jnp.sum(q * kd, axis=1, keepdims=True)
        reading = reading + (affinity * g[:, delta:delta + 1]) * vd
    scale = lax.rsqrt(jnp.mean(reading * reading, axis=1, keepdims=True) + EPSILON)
    out_ref[...] = (reading * scale).astype(BF16)


def local(query_rows, key_rows, value_rows, decay_rates, valid_blocks, step_queries, step_keys, step_values, step_rates, row_session):
    tokens, width = query_rows.shape[1:]
    heads = decay_rates.shape[2]
    blocks = tokens // BLK
    pairs = heads // 2
    queries, keys, values, rates = query_rows[0], key_rows[0], value_rows[0], decay_rates[0]
    smem = pl.BlockSpec(memory_space=pltpu.SMEM)
    pair_block = pl.BlockSpec((tokens, 2 * DH), lambda p: (0, p))
    rate_block = pl.BlockSpec((tokens, heads), lambda p: (0, 0))
    mid_block = pl.BlockSpec((2, blocks - 1, DH, DH), lambda p: (p, 0, 0, 0))
    end_block = pl.BlockSpec((2, DH + 8, DH), lambda p: (p, 0, 0))
    params = pltpu.CompilerParams(vmem_limit_bytes=48 << 20)

    row_count, steps, share = step_queries.shape
    share_heads = share // DH
    sessions = lax.axis_size("sess")

    def by_head(data):
        return data.reshape(row_count, steps, share_heads, DH).transpose(0, 2, 1, 3).reshape(row_count, share_heads * steps, DH)

    named = row_session[:, 0][None, :] == jnp.arange(sessions, dtype=jnp.int32)[:, None]
    place = jnp.sum(jnp.where(named, jnp.arange(row_count, dtype=jnp.int32)[None, :], 0), axis=1)
    q_rows = by_head(step_queries)
    slots = jnp.where(named.any(axis=1)[:, None, None], q_rows[place], 0)
    arrived = lax.all_to_all(slots, "sess", 0, 0, tiled=True)

    mid, end = pl.pallas_call(
        functools.partial(states_kernel, heads, blocks),
        grid=(pairs,),
        out_shape=(jax.ShapeDtypeStruct((heads, blocks - 1, DH, DH), F32), jax.ShapeDtypeStruct((heads, DH + 8, DH), F32)),
        in_specs=[smem, rate_block, pair_block, pair_block],
        out_specs=(mid_block, end_block),
        scratch_shapes=[pltpu.VMEM((blocks, BLK, 128), BF16)],
        compiler_params=params,
    )(valid_blocks, rates, keys, values)
    prefix = lax.ppermute(end, "ctx", [(0, 1)])
    latter = lax.ppermute(end[:share_heads], "ctx", [(1, 0)])
    mine = lax.dynamic_slice_in_dim(end, lax.axis_index("ctx") * share_heads, share_heads, 0)
    other = jnp.where(lax.axis_index("ctx") == 0, latter, prefix[share_heads:])

    state_block = pl.BlockSpec((4, DH + 8, DH), lambda p: (p, 0, 0))
    slot_block = pl.BlockSpec((sessions, 16, DH), lambda p: (0, p, 0))
    projected = pl.pallas_call(
        project_kernel,
        grid=(share_heads // 4,),
        out_shape=jax.ShapeDtypeStruct((sessions, share_heads * steps, DH), BF16),
        in_specs=[slot_block, state_block, state_block],
        out_specs=slot_block,
        compiler_params=params,
    )(arrived, mine, other)
    back = lax.all_to_all(projected, "sess", 0, 0, tiled=True)

    prefill_out = pl.pallas_call(
        functools.partial(outputs_kernel, heads, blocks),
        grid=(pairs,),
        out_shape=jax.ShapeDtypeStruct((tokens, width), BF16),
        in_specs=[smem, rate_block, pair_block, pair_block, pair_block, mid_block, end_block],
        out_specs=pair_block,
        scratch_shapes=[pltpu.VMEM((blocks, BLK, 128), BF16), pltpu.VMEM((blocks, heads, BLK), F32)],
        compiler_params=params,
    )(valid_blocks, rates, queries, keys, values, mid, prefix)

    log_factor = jnp.cumsum(-step_rates.astype(F32), axis=1).transpose(0, 2, 1)
    factors = []
    for delta in range(steps):
        gap = log_factor[:, :, delta:] - log_factor[:, :, :steps - delta]
        factors.append(jnp.pad(jnp.exp(gap), ((0, 0), (0, 0), (delta, 0))))
    factors.append(jnp.exp(log_factor))
    gains = jnp.stack(factors, axis=-1).reshape(row_count * share_heads * steps, steps + 1)

    flat = (row_count * share_heads * steps, DH)
    part = 256
    flat_block = pl.BlockSpec((part, DH), lambda p: (p, 0))
    decoded = pl.pallas_call(
        decode_kernel,
        grid=(flat[0] // part,),
        out_shape=jax.ShapeDtypeStruct(flat, BF16),
        in_specs=[flat_block] * 4 + [pl.BlockSpec((part, steps + 1), lambda p: (p, 0))],
        out_specs=flat_block,
        compiler_params=params,
    )(q_rows.reshape(flat), by_head(step_keys).reshape(flat), by_head(step_values).reshape(flat), back[row_session[:, 0]].reshape(flat), gains)
    decode_out = decoded.reshape(row_count, share_heads, steps, DH).transpose(0, 2, 1, 3).reshape(row_count, steps, share)
    return prefill_out[None], decode_out


def solution(mesh):
    long, step = P("sess", "ctx", None), P("sess", None, "ctx")
    return jax.shard_map(
        local,
        mesh=mesh,
        in_specs=(long, long, long, long, P("sess"), step, step, step, step, P("sess", None)),
        out_specs=(long, step),
        check_vma=False,
    )
```

time: 558 us -> 126 us (0.23)
  waiting for transfers between devices: 230 us -> 17 us
  matrix products: 130 us -> 0 us
  local copies, waits for them, and re-layouts: 88.1 us -> 23.3 us
  loops' own time: 62.2 us -> 0 us
  Pallas kernels: 0 us -> 55.2 us
  other arithmetic: 27.7 us -> 3.96 us
  starting transfers between devices: 0.12 us -> 23.2 us
  between operations: 14.7 us -> 1.53 us
    all_gather x2 -> x0, waiting for transfers between devices: 202 us -> none  [the longest x1 184 us: local(): lax.all_gather(session_heads[None], 'sess', axis=0, tiled=True)]
    dot_general x43 -> x0, matrix products: 130 us -> none  [the longest x32 77.5 us: project_row(): jnp.einsum('shd,hde->she', row_queries.astype(jnp.float32), picked, preci...]
    another operation x1 -> x0, loops' own time: 62.2 us -> none  [local(): projected = lax.map(project_row, (row_session[:, 0], split_queries))]
    pallas_call x0 -> x4, Pallas kernels: none -> 55.2 us  [the longest x1 27 us: local(): pl.pallas_call(functools.partial(outputs_kernel, heads, blocks), grid=(pa...]
    psum x1 -> x0, waiting for transfers between devices: 28.2 us -> none  [from_root(): return lax.psum(kept, axis)]
    unnamed x25 -> x22, local copies, waits for them, and re-layouts: 30.3 us -> 8.45 us
    dynamic_slice x33 -> x0, local copies, waits for them, and re-layouts: 20.9 us -> none  [the longest x32 18.6 us: local(): projected = lax.map(project_row, (row_session[:, 0], split_queries))]
    all_to_all x0 -> x2, starting transfers between devices: none -> 17.4 us  [the longest x1 11.9 us: local(): arrived = lax.all_to_all(slots, 'sess', 0, 0, tiled=True)]
  transfers between devices with their start and end apart: 3 -> 4, of which waited for: 3 -> 1; matrix products, arithmetic and copies ran while one was open for 17% -> 14% of each run, Pallas kernels for 0% -> 22%
where the time goes in v1:
time: 126 us; the launch traced here: 124 us
  Pallas kernels  55.2 us (44%)
  local copies, waits for them, and re-layouts  23.3 us (18%)
  starting transfers between devices  23.2 us (18%)
  waiting for transfers between devices  17 us (13%)
  other arithmetic  3.96 us (3%)
  between operations  1.53 us (1%)
    pallas_call x1, Pallas kernels, local(): pl.pallas_call(functools.partial(outputs_kernel, heads, blocks), grid=(pa...  27 us
    pallas_call x1, Pallas kernels, local(): pl.pallas_call(functools.partial(states_kernel, heads, blocks), grid=(pai...  17.9 us
    all_to_all x1, waiting for transfers between devices, local(): arrived = lax.all_to_all(slots, 'sess', 0, 0, tiled=True)  17 us
    all_to_all x1, starting transfers between devices, local(): arrived = lax.all_to_all(slots, 'sess', 0, 0, tiled=True)  11.9 us
    unnamed x22, local copies, waits for them, and re-layouts  8.45 us
    pallas_call x1, Pallas kernels, local(): pl.pallas_call(decode_kernel, grid=(flat[0] // part,), out_shape=jax.Shap...  6.94 us
    all_to_all x1, starting transfers between devices, local(): back = lax.all_to_all(projected, 'sess', 0, 0, tiled=True)  5.51 us
    another operation x7, local copies, waits for them, and re-layouts, local(): jnp.stack(factors, axis=-1)  5.14 us
  transfers between devices with their start and end apart: 4, of which 1 were waited for; matrix products, arithmetic and copies ran while one was open for 14% of the time, Pallas kernels for 22%

profile of v1, /device:TPU:1, one launch (start us, length us, event | category | flops | bytes accessed | tf_op | source)
XLA Modules:
  0.0 124.2 jit_solution(2511953524271927102)
XLA Ops:
  0.6 1.1 copy.48
  2.3 17.9 %shard_map.113 = (f32[32,2,128,128]{3,2,1,0:T(8,128)}, f32[32,136,128]{2,1,0:T(8,128)}) custom-call(s32[1]{0:T(128)S(6)} %copy.62.valid_ref, f32[768,32]{1,0:T(8,128)S(1)} %bitcast.39, bf16[768,4096]{1,0:T(8,128)(2,1)} %bitcast.44, bf16[768,4096]{1,0:T(8,128)(2,1)} %bitcast.46), custom_call_target="tpu_custom_call" | custom-call | tf_op jit(solution)/shard_map/pallas_call | solution.py:191
  20.2 1.3 %collective-permute-start = (f32[32,136,128]{2,1,0:T(8,128)}, f32[32,136,128]{2,1,0:T(8,128)S(1)}, u32[]{:S(2)}, u32[]{:S(2)}) collective-permute-start(f32[32,136,128]{2,1,0:T(8,128)} %get-tuple-element.5), channel_id=1, source_target_pairs={{0,64},{1,65},{2,66},{3,67},{4,68},{5,69},{6,70},{7,71},{8,72},{9,... | collective-permute-start | bytes 6684680 | tf_op jit(solution)/shard_map/ppermute | solution.py:200
  21.5 3.1 %fusion.8 = (f32[16,136,128]{2,1,0:T(8,128)}, f32[16,136,128]{2,1,0:T(8,128)}) fusion(f32[32,136,128]{2,1,0:T(8,128)} %get-tuple-element.5, s32[]{:T(128)S(6)} %select_n.36), kind=kLoop, calls=%fused_computation.24 | loop fusion | bytes 4456452 | tf_op jit(solution)/shard_map/slice | solution.py:201
  24.7 4.5 %collective-permute-start.1 = (f32[16,136,128]{2,1,0:T(8,128)}, f32[16,136,128]{2,1,0:T(8,128)}, u32[]{:S(2)}, u32[]{:S(2)}) collective-permute-start(f32[16,136,128]{2,1,0:T(8,128)} %get-tuple-element.6), channel_id=1, source_target_pairs={{64,0},{65,1},{66,2},{67,3},{68,4},{69,5},{70,6},{71,7},{72,8},{73... | collective-permute-start | bytes 3342344 | tf_op jit(solution)/shard_map/ppermute | solution.py:201
  29.3 1.8 %gather_fusion = bf16[64,64,128]{2,1,0:T(8,128)(2,1)} fusion(bf16[32,64,128]{2,1,0:T(8,128)(2,1)S(1)} %bitcast.37, s32[1024]{0:T(1024)S(1)} %pad_clamp_fusion.1), kind=kCustom, calls=%fused_computation | custom fusion | bytes 2097408 | tf_op jit(solution)/shard_map/gather | solution.py:188
  31.1 2.4 %broadcast_select_fusion = bf16[64,64,128]{2,1,0:T(8,128)(2,1)} fusion(bf16[64,64,128]{2,1,0:T(8,128)(2,1)} %gather_fusion, pred[64]{0:T(512)(128)(4,1)S(1)} %fusion.4), kind=kLoop, calls=%fused_computation.4 | loop fusion | flops 524288 | bytes 2097216 | tf_op jit(solution)/shard_map/jit(_where)/select_n | solution.py:188
  33.6 11.9 %all-to-all-start = ((bf16[64,64,128]{2,1,0:T(8,128)(2,1)}), bf16[64,64,128]{2,1,0:T(8,128)(2,1)}, u32[]{:S(2)}, u32[]{:S(2)}) async-start(bf16[64,64,128]{2,1,0:T(8,128)(2,1)} %broadcast_select_fusion), calls=%async_computation | async-start | bytes 2097152 | tf_op jit(solution)/shard_map/all_to_all | solution.py:189
  45.5 1.1 slice_select_fusion.other_ref
  46.6 17.0 %all-to-all-done.x_ref = bf16[64,64,128]{2,1,0:T(8,128)(2,1)} async-done(((bf16[64,64,128]{2,1,0:T(8,128)(2,1)}), bf16[64,64,128]{2,1,0:T(8,128)(2,1)}, u32[]{:S(2)}, u32[]{:S(2)}) %all-to-all-start) | async-done | bytes 1048608 | tf_op jit(solution)/shard_map/all_to_all | solution.py:189
  63.6 1.2 %copy-done.1 = f32[16,136,128]{2,1,0:T(8,128)S(1)} copy-done((f32[16,136,128]{2,1,0:T(8,128)S(1)}, f32[16,136,128]{2,1,0:T(8,128)}, u32[]{:S(2)}) %copy-start.1) | copy-done | bytes 1114136
  64.9 1.2 %copy-done.2 = f32[16,136,128]{2,1,0:T(8,128)S(1)} copy-done((f32[16,136,128]{2,1,0:T(8,128)S(1)}, f32[16,136,128]{2,1,0:T(8,128)}, u32[]{:S(2)}) %copy-start.2) | copy-done | bytes 1114136
  66.1 3.4 %shard_map.115 = bf16[64,64,128]{2,1,0:T(8,128)(2,1)S(1)} custom-call(bf16[64,64,128]{2,1,0:T(8,128)(2,1)} %all-to-all-done.x_ref, f32[16,136,128]{2,1,0:T(8,128)S(1)} %copy-done.1, f32[16,136,128]{2,1,0:T(8,128)S(1)} %copy-done.2), custom_call_target="tpu_custom_call" | custom-call | tf_op jit(solution)/shard_map/pallas_call | solution.py:207
  70.6 5.5 %all-to-all-start.1 = ((bf16[64,64,128]{2,1,0:T(8,128)(2,1)}), bf16[64,64,128]{2,1,0:T(8,128)(2,1)}, u32[]{:S(2)}, u32[]{:S(2)}) async-start(bf16[64,64,128]{2,1,0:T(8,128)(2,1)} %copy-done.4), calls=%async_computation.1 | async-start | bytes 2097152 | tf_op jit(solution)/shard_map/all_to_all | solution.py:215
  77.3 1.1 stack.19
  79.5 1.1 stack.20
  81.7 1.1 stack.21
  83.7 1.4 %copy.57.g_ref = f32[2048,5]{1,0:T(8,128)} copy(f32[2048,5]{0,1:T(8,128)S(1)} %stack.23) | data formatting | bytes 81920 | tf_op jit(solution)/shard_map/stack | solution.py:233
  85.1 27.0 %shard_map.114 = bf16[768,4096]{1,0:T(8,128)(2,1)} custom-call(s32[1]{0:T(128)S(6)} %copy.62.valid_ref, f32[768,32]{1,0:T(8,128)S(1)} %bitcast.40, bf16[768,4096]{1,0:T(8,128)(2,1)} %bitcast.48, bf16[768,4096]{1,0:T(8,128)(2,1)} %bitcast.45, bf16[768,4096]{1,0:T(8,128)(2,1)} %bitcast.47, f32[32,2,128,128]{3,2,1,0:T(8,128)} %get-tuple-element.4.mid_ref, ...), custom_call_target="tpu_custom_call" | custom-call | tf_op jit(solution)/shard_map/pallas_call | solution.py:217
  112.1 1.9 %gather_fusion.1 = bf16[32,64,128]{2,1,0:T(8,128)(2,1)S(1)} fusion(bf16[64,64,128]{2,1,0:T(8,128)(2,1)} %all-to-all-done.1, s32[1024]{0:T(1024)S(1)} %pad_clamp_fusion), kind=kCustom, calls=%fused_computation.1 | custom fusion | bytes 1048704 | tf_op jit(solution)/shard_map/gather | solution.py:245
  114.0 1.2 copy-done.3
  115.2 1.0 copy-done.5
  116.2 1.0 copy-done.6
  117.3 6.9 %shard_map.116 = bf16[2048,128]{1,0:T(8,128)(2,1)} custom-call(bf16[2048,128]{1,0:T(8,128)(2,1)S(1)} %bitcast.38, bf16[2048,128]{1,0:T(8,128)(2,1)S(1)} %bitcast.42, bf16[2048,128]{1,0:T(8,128)(2,1)S(1)} %bitcast.43, bf16[2048,128]{1,0:T(8,128)(2,1)S(1)} %bitcast.41, f32[2048,5]{1,0:T(8,128)S(1)} %copy-done.3), custom_call_target="tpu_custom_call" | custom-call | tf_op jit(solution)/shard_map/pallas_call | solution.py:238
  (37 shorter events, 5.4 us)
Async XLA Ops:
  20.2 25.3 %collective-permute-start = (f32[32,136,128]{2,1,0:T(8,128)}, f32[32,136,128]{2,1,0:T(8,128)S(1)}, u32[]{:S(2)}, u32[]{:S(2)}) collective-permute-start(f32[32,136,128]{2,1,0:T(8,128)} %get-tuple-element.5), channel_id=1, source_target_pairs={{0,64},{1,65},{2,66},{3,67},{4,68},{5,69},{6,70},{7,71},{8,72},{9,... | collective-permute-start | bytes 6684680 | tf_op jit(solution)/shard_map/ppermute | solution.py:200
  21.5 7.6 %copy-start.8 = (s32[32,1]{0,1:T(1,128)S(1)}, s32[32,1]{0,1:T(1,128)}, u32[]{:S(2)}) copy-start(s32[32,1]{0,1:T(1,128)} %param.19) | copy-start | bytes 388
  21.5 7.7 %copy-start = (bf16[32,4,2048]{2,1,0:T(4,128)(2,1)S(1)}, bf16[32,4,2048]{2,1,0:T(4,128)(2,1)}, u32[]{:S(2)}) copy-start(bf16[32,4,2048]{2,1,0:T(4,128)(2,1)} %param.15) | copy-start | bytes 1572868
  24.7 20.8 %collective-permute-start.1 = (f32[16,136,128]{2,1,0:T(8,128)}, f32[16,136,128]{2,1,0:T(8,128)}, u32[]{:S(2)}, u32[]{:S(2)}) collective-permute-start(f32[16,136,128]{2,1,0:T(8,128)} %get-tuple-element.6), channel_id=1, source_target_pairs={{64,0},{65,1},{66,2},{67,3},{68,4},{69,5},{70,6},{71,7},{72,8},{73... | collective-permute-start | bytes 3342344 | tf_op jit(solution)/shard_map/ppermute | solution.py:201
  33.6 30.1 %all-to-all-start = ((bf16[64,64,128]{2,1,0:T(8,128)(2,1)}), bf16[64,64,128]{2,1,0:T(8,128)(2,1)}, u32[]{:S(2)}, u32[]{:S(2)}) async-start(bf16[64,64,128]{2,1,0:T(8,128)(2,1)} %broadcast_select_fusion), calls=%async_computation | async-start | bytes 2097152 | tf_op jit(solution)/shard_map/all_to_all | solution.py:189
  63.6 1.2 %copy-start.1 = (f32[16,136,128]{2,1,0:T(8,128)S(1)}, f32[16,136,128]{2,1,0:T(8,128)}, u32[]{:S(2)}) copy-start(f32[16,136,128]{2,1,0:T(8,128)} %get-tuple-element.7.mine_ref) | copy-start | bytes 3342340
  64.9 1.2 %copy-start.2 = (f32[16,136,128]{2,1,0:T(8,128)S(1)}, f32[16,136,128]{2,1,0:T(8,128)}, u32[]{:S(2)}) copy-start(f32[16,136,128]{2,1,0:T(8,128)} %slice_select_fusion.other_ref) | copy-start | bytes 3342340
  66.1 10.0 %copy-start.7 = (bf16[32,4,16]{0,2,1:T(8,128)(2,1)S(1)}, bf16[32,4,16]{0,2,1:T(8,128)(2,1)}, u32[]{:S(2)}) copy-start(bf16[32,4,16]{0,2,1:T(8,128)(2,1)} %param.18) | copy-start | bytes 12292
  69.6 1.0 copy-start.4
  70.6 41.5 %all-to-all-start.1 = ((bf16[64,64,128]{2,1,0:T(8,128)(2,1)}), bf16[64,64,128]{2,1,0:T(8,128)(2,1)}, u32[]{:S(2)}, u32[]{:S(2)}) async-start(bf16[64,64,128]{2,1,0:T(8,128)(2,1)} %copy-done.4), calls=%async_computation.1 | async-start | bytes 2097152 | tf_op jit(solution)/shard_map/all_to_all | solution.py:215
  113.9 1.2 copy-start.3
  115.2 1.0 copy-start.5
  116.2 1.0 copy-start.6

commit v2 on v1

v2 whole, which is shorter than its diff:
```python
import functools

import jax
import jax.numpy as jnp
from jax import lax
from jax.experimental import pallas as pl
from jax.experimental.pallas import tpu as pltpu
from jax.sharding import PartitionSpec as P

BLK = 256
DH = 128
EPSILON = 1e-06
F32 = jnp.float32
BF16 = jnp.bfloat16
HIGH = lax.Precision.HIGHEST
MESH = pl.DeviceIdType.MESH


def dot(a, b, dims=((1,), (0,)), precision=None):
    return lax.dot_general(a, b, (dims, ((), ())), precision=precision, preferred_element_type=F32)


def iota(shape, axis):
    return lax.broadcasted_iota(jnp.int32, shape, axis)


def prepare(rates, live, heads):
    lanes = iota((heads, 128), 1)
    copies = (lax.rem(lanes, heads) == iota((heads, 128), 0)).astype(F32)
    lower = (iota((BLK, BLK), 0) >= iota((BLK, BLK), 1)).astype(F32)
    wide = dot(rates * live, copies, precision=HIGH)
    running = dot(lower, wide, precision=HIGH)
    first = running.astype(BF16).astype(F32)
    second = (running - first).astype(BF16).astype(F32)
    third = running - first - second
    group = lax.div(iota((BLK, 128), 1), heads)
    parts = jnp.where(group == 0, first, jnp.where(group == 1, second, jnp.where(group == 2, third, 0.0)))
    return parts.astype(BF16), running.T


def live_factor(valid_ref, j, blocks):
    return (lax.axis_index("ctx") * blocks + j < valid_ref[0]).astype(F32)


def fused_kernel(
    sizes,
    valid_ref, place_ref, session_ref, rates_ref, q_hbm, k_hbm, v_hbm, sq_hbm, sk_hbm, sv_hbm, gains_hbm,
    out_hbm, decoded_ref,
    qb, kb, vb, sq, sk, sv, gains, slots, arrived, projected, back, recent,
    states, other_states, before, decays, other_decays, parts, turned, spread,
    load_sem, store_sem, step_sem, send_sem, recv_sem, back_send_sem, back_recv_sem, pair_send_sem, pair_recv_sem,
):
    heads, blocks, sessions, rows_here, steps, (side_z, side_y, side_x) = sizes
    share = heads // 2
    groups = heads // 4
    core = lax.axis_index("ctx")
    me = lax.axis_index("sess")
    my_x, my_y, my_z = lax.rem(me, side_x), lax.rem(lax.div(me, side_x), side_y), lax.div(me, side_x * side_y)

    def peer(i):
        px = lax.rem(my_x + lax.rem(i, side_x), side_x)
        py = lax.rem(my_y + lax.rem(lax.div(i, side_x), side_y), side_y)
        pz = lax.rem(my_z + lax.div(i, side_x * side_y), side_z)
        return (pz * side_y + py) * side_x + px

    def block_rows(j):
        return pl.ds(pl.multiple_of(j * BLK, BLK), BLK)

    def load(which, hbm, buffer, j):
        return pltpu.make_async_copy(hbm.at[block_rows(j)], buffer.at[block_rows(j)], load_sem.at[which, j])

    def store(j):
        return pltpu.make_async_copy(qb.at[block_rows(j)], out_hbm.at[block_rows(j)], store_sem.at[j])

    small = [
        pltpu.make_async_copy(a, b, step_sem.at[i])
        for i, (a, b) in enumerate(((sq_hbm, sq), (sk_hbm, sk), (sv_hbm, sv), (gains_hbm, gains)))
    ]
    small[0].start()
    for j in range(blocks):
        load(0, k_hbm, kb, j).start()
        load(1, v_hbm, vb, j).start()
    for copy in small[1:]:
        copy.start()
    for j in range(blocks):
        load(2, q_hbm, qb, j).start()

    barrier = pltpu.get_barrier_semaphore()
    pl.semaphore_signal(barrier, inc=1, device_id=(1 - core, me), device_id_type=MESH)

    def greet(i, carry):
        pl.semaphore_signal(barrier, inc=1, device_id=(core, peer(i)), device_id_type=MESH)
        return carry

    lax.fori_loop(1, sessions, greet, 0)

    small[0].wait()

    def fill(s, carry):
        row = place_ref[s]
        slots[s] = jnp.where(row < rows_here, sq[jnp.minimum(row, rows_here - 1)], jnp.zeros(sq.shape[1:], BF16))
        return carry

    lax.fori_loop(0, sessions, fill, 0)
    arrived[me] = slots[me]
    pl.semaphore_wait(barrier, sessions)

    def dispatch(i):
        return pltpu.make_async_remote_copy(
            src_ref=slots.at[peer(i)], dst_ref=arrived.at[me], send_sem=send_sem.at[i], recv_sem=recv_sem.at[i],
            device_id=(core, peer(i)), device_id_type=MESH)

    def give_back(i):
        return pltpu.make_async_remote_copy(
            src_ref=projected.at[peer(i)], dst_ref=back.at[me], send_sem=back_send_sem.at[i], recv_sem=back_recv_sem.at[i],
            device_id=(core, peer(i)), device_id_type=MESH)

    def each_peer(act):
        def lap(i, carry):
            act(i)
            return carry
        lax.fori_loop(1, sessions, lap, 0)

    each_peer(lambda i: dispatch(i).start())

    for j in range(blocks):
        block_parts, block_turned = prepare(rates_ref[j * BLK:(j + 1) * BLK, :], live_factor(valid_ref, j, blocks), heads)
        parts[j] = block_parts
        turned[j] = block_turned[0:heads, :]

    def spread_group(g, carry):
        row, lane = iota((128, 4 * DH), 0), iota((128, 4 * DH), 1)
        wanted = g * 4 + lax.div(lane, DH)
        chosen = (lax.rem(row, heads) == wanted) & (row < 3 * heads)
        spread[:, pl.ds(pl.multiple_of(g * 4 * DH, 4 * DH), 4 * DH)] = chosen.astype(F32).astype(BF16)
        return carry

    lax.fori_loop(0, groups, spread_group, 0)
    states[0] = jnp.zeros(states.shape[1:], F32)
    before[0] = jnp.zeros(before.shape[1:], F32)

    def group_cols(g):
        return pl.ds(pl.multiple_of(g * 4 * DH, 4 * DH), 4 * DH)

    def state_block(j, carry):
        load(0, k_hbm, kb, j).wait()
        load(1, v_hbm, vb, j).wait()
        live = live_factor(valid_ref, j, blocks)

        def state_group(g, carry):
            rows, cols = block_rows(j), group_cols(g)
            running = dot(parts[j], spread[:, cols])
            last = running[BLK - 1:BLK, :]
            weighted = (kb[rows, cols].astype(F32) * (jnp.exp(running - last) * live)).astype(BF16)
            decay = jnp.exp(-last)
            values = vb[rows, cols]
            before[j + 1, :, cols] = before[j, :, cols] + last
            for one in range(4):
                h = g * 4 + one
                lanes = slice(one * DH, (one + 1) * DH)
                grown = dot(weighted[:, lanes], values[:, lanes], ((0,), (0,)))
                states[j + 1, h] = decay[:, lanes] * states[j, h] + grown
            return carry

        return lax.fori_loop(0, groups, state_group, carry)

    lax.fori_loop(0, blocks, state_block, 0)
    for h in range(heads):
        decays[h] = jnp.exp(-before[blocks, :, h * DH:(h + 1) * DH])

    theirs, ours = pl.multiple_of((1 - core) * share, share), pl.multiple_of(core * share, share)
    exchange = [
        pltpu.make_async_remote_copy(
            src_ref=a, dst_ref=b, send_sem=pair_send_sem.at[i], recv_sem=pair_recv_sem.at[i],
            device_id=(1 - core, me), device_id_type=MESH)
        for i, (a, b) in enumerate((
            (decays, other_decays),
            (states.at[blocks, pl.ds(theirs, share)], other_states.at[pl.ds(theirs, share)]),
            (states.at[blocks, pl.ds(ours, share)], other_states.at[pl.ds(ours, share)]),
        ))
    ]
    for copy in exchange:
        copy.start()

    for copy in small[1:]:
        copy.wait()

    def recent_part(p, carry):
        q, k, v = (ref[pl.ds(p * 4, 4)].reshape(4 * share * steps, DH).astype(F32) for ref in (sq, sk, sv))
        rows = pl.ds(pl.multiple_of(p * 4 * share * steps, 4 * share * steps), 4 * share * steps)
        g = gains[rows, :]
        total = None
        for delta in range(steps):
            kd = k if delta == 0 else pltpu.roll(k, delta, 0)
            vd = v if delta == 0 else pltpu.roll(v, delta, 0)
            term = (jnp.sum(q * kd, axis=1, keepdims=True) * g[:, delta:delta + 1]) * vd
            total = term if total is None else total + term
        recent[rows, :] = total
        return carry

    lax.fori_loop(0, rows_here // 4, recent_part, 0)

    for copy in exchange:
        copy.wait()

    half = BLK // 2
    first_core = core == 0

    def output_block(j):
        load(2, q_hbm, qb, j).wait()
        live = live_factor(valid_ref, j, blocks)

        def output_group(g, carry):
            rows, cols = block_rows(j), group_cols(g)
            running = dot(parts[j], spread[:, cols])
            from_start = jnp.exp(-running)
            q4, k4, v4 = qb[rows, cols], kb[rows, cols], vb[rows, cols]
            lower = iota((half, half), 0) >= iota((half, half), 1)
            entry = jnp.exp(-before[j, 0:1, cols])
            for one in range(4):
                h = g * 4 + one
                lanes = slice(one * DH, (one + 1) * DH)
                row = turned[j, pl.ds(h, 1), :]
                run = running[:, lanes]
                q, k, v = q4[:, lanes], k4[:, lanes], v4[:, lanes]
                scores0 = dot(q[:half], k[:half], ((1,), (1,)))
                scores1 = dot(q[half:], k, ((1,), (1,)))
                mixed0 = jnp.where(lower, scores0 * jnp.exp(row[:, :half] - run[:half]), 0.0).astype(BF16)
                mixed10 = scores1[:, :half] * jnp.exp(row[:, :half] - run[half:])
                mixed11 = jnp.where(lower, scores1[:, half:] * jnp.exp(row[:, half:] - run[half:]), 0.0)
                mixed1 = jnp.concatenate([mixed10, mixed11], axis=1).astype(BF16)
                within = jnp.concatenate([dot(mixed0, v[:half]), dot(mixed1, v)], axis=0)
                prefix = jnp.where(first_core, 0.0, entry[:, lanes] * other_states[h])
                entering = (prefix + states[j, h]).astype(BF16)
                mix = within + from_start[:, lanes] * dot(q, entering)
                scale = lax.rsqrt(jnp.mean(mix * mix, axis=1, keepdims=True) + EPSILON) * live
                qb[rows, pl.ds(pl.multiple_of(h * DH, DH), DH)] = (mix * scale).astype(BF16)
            return carry

        lax.fori_loop(0, groups, output_group, 0)
        store(j).start()

    output_block(0)

    each_peer(lambda i: dispatch(i).wait())

    def project(quad, carry):
        part = pl.ds(pl.multiple_of(quad * 16, 16), 16)
        x = arrived[:, part, :].reshape(sessions * 16, DH)
        doubled = jnp.concatenate([x, x], axis=1)
        position = lax.div(lax.rem(iota((sessions * 16, DH), 0), 16), 4)
        chosen = None
        for two in range(2):
            columns = []
            for one in range(2):
                h = core * share + quad * 4 + two * 2 + one
                mine, other = states[blocks, h], other_states[h]
                earlier = jnp.where(first_core, mine, other)
                latter = jnp.where(first_core, other, mine)
                decay = jnp.where(first_core, other_decays[h, 0:1, :], decays[h, 0:1, :])
                final = decay * earlier + latter
                upper = final.astype(BF16)
                rest = (final - upper.astype(F32)).astype(BF16)
                columns.append(jnp.concatenate([upper, rest], axis=0))
            product = dot(doubled, jnp.concatenate(columns, axis=1))
            for one in range(2):
                piece = product[:, one * DH:(one + 1) * DH]
                chosen = piece if chosen is None else jnp.where(position == two * 2 + one, piece, chosen)
        projected[:, part, :] = chosen.astype(BF16).reshape(sessions, 16, DH)
        return carry

    lax.fori_loop(0, share // 4, project, 0)
    back[me] = projected[me]
    each_peer(lambda i: give_back(i).start())

    def other_blocks(j, carry):
        output_block(j)
        return carry

    lax.fori_loop(1, blocks, other_blocks, 0)

    each_peer(lambda i: give_back(i).wait())

    def finish(p, carry):
        rows = pl.ds(pl.multiple_of(p * 4 * share * steps, 4 * share * steps), 4 * share * steps)
        pieces = [back[session_ref[p * 4 + i]].astype(F32) for i in range(4)]
        reading = gains[rows, steps:steps + 1] * jnp.concatenate(pieces, axis=0) + recent[rows, :]
        scale = lax.rsqrt(jnp.mean(reading * reading, axis=1, keepdims=True) + EPSILON)
        decoded_ref[rows, :] = (reading * scale).astype(BF16)
        return carry

    lax.fori_loop(0, rows_here // 4, finish, 0)
    for j in range(blocks):
        store(j).wait()


def local(side, query_rows, key_rows, value_rows, decay_rates, valid_blocks, step_queries, step_keys, step_values, step_rates, row_session):
    tokens, width = query_rows.shape[1:]
    heads = decay_rates.shape[2]
    blocks = tokens // BLK
    row_count, steps, share_width = step_queries.shape
    share = share_width // DH
    sessions = lax.axis_size("sess")

    def by_head(data):
        return data.reshape(row_count, steps, share, DH).transpose(0, 2, 1, 3).reshape(row_count, share * steps, DH)

    named = row_session[:, 0][None, :] == jnp.arange(sessions, dtype=jnp.int32)[:, None]
    place = jnp.min(jnp.where(named, jnp.arange(row_count, dtype=jnp.int32)[None, :], row_count), axis=1)

    log_factor = jnp.cumsum(-step_rates.astype(F32), axis=1).transpose(0, 2, 1)
    factors = []
    for delta in range(steps):
        gap = log_factor[:, :, delta:] - log_factor[:, :, :steps - delta]
        factors.append(jnp.pad(jnp.exp(gap), ((0, 0), (0, 0), (delta, 0))))
    factors.append(jnp.exp(log_factor))
    flat_rows = row_count * share * steps
    gains = jnp.stack(factors, axis=-1).reshape(flat_rows, steps + 1)

    smem = pl.BlockSpec(memory_space=pltpu.SMEM)
    vmem = pl.BlockSpec(memory_space=pltpu.VMEM)
    hbm = pl.BlockSpec(memory_space=pl.ANY)
    slot = (share * steps, DH)
    dma = pltpu.SemaphoreType.DMA
    prefill_out, decoded = pl.pallas_call(
        functools.partial(fused_kernel, (heads, blocks, sessions, row_count, steps, side)),
        out_shape=(jax.ShapeDtypeStruct((tokens, width), BF16), jax.ShapeDtypeStruct((flat_rows, DH), BF16)),
        in_specs=[smem, smem, smem, vmem] + [hbm] * 7,
        out_specs=(hbm, vmem),
        scratch_shapes=[
            pltpu.VMEM((tokens, width), BF16), pltpu.VMEM((tokens, width), BF16), pltpu.VMEM((tokens, width), BF16),
            pltpu.VMEM((row_count,) + slot, BF16), pltpu.VMEM((row_count,) + slot, BF16), pltpu.VMEM((row_count,) + slot, BF16),
            pltpu.VMEM((flat_rows, steps + 1), F32),
            pltpu.VMEM((sessions,) + slot, BF16), pltpu.VMEM((sessions,) + slot, BF16),
            pltpu.VMEM((sessions,) + slot, BF16), pltpu.VMEM((sessions,) + slot, BF16),
            pltpu.VMEM((flat_rows, DH), F32),
            pltpu.VMEM((blocks + 1, heads, DH, DH), F32), pltpu.VMEM((heads, DH, DH), F32),
            pltpu.VMEM((blocks + 1, 8, width), F32), pltpu.VMEM((heads, 8, DH), F32), pltpu.VMEM((heads, 8, DH), F32),
            pltpu.VMEM((blocks, BLK, 128), BF16), pltpu.VMEM((blocks, heads, BLK), F32), pltpu.VMEM((128, width), BF16),
            dma((3, blocks)), dma((blocks,)), dma((4,)), dma((sessions,)), dma((sessions,)), dma((sessions,)), dma((sessions,)),
            dma((3,)), dma((3,)),
        ],
        compiler_params=pltpu.CompilerParams(collective_id=0, has_side_effects=True, vmem_limit_bytes=56 << 20),
    )(valid_blocks, place, row_session[:, 0], decay_rates[0], query_rows[0], key_rows[0], value_rows[0],
      by_head(step_queries), by_head(step_keys), by_head(step_values), gains)
    decode_out = decoded.reshape(row_count, share, steps, DH).transpose(0, 2, 1, 3).reshape(row_count, steps, share_width)
    return prefill_out[None], decode_out


def solution(mesh):
    long, step = P("sess", "ctx", None), P("sess", None, "ctx")
    devices = mesh.shape["sess"]
    side = round(devices ** (1 / 3))
    sides = (side, side, side) if side ** 3 == devices else (1, 1, devices)
    return jax.shard_map(
        functools.partial(local, sides),
        mesh=mesh,
        in_specs=(long, long, long, long, P("sess"), step, step, step, step, P("sess", None)),
        out_specs=(long, step),
        check_vma=False,
    )
```

time: 126 us -> 84.7 us (0.67); the launches traced: 124 us -> 84.5 us
  starting transfers between devices: 23.2 us -> 0 us
  waiting for transfers between devices: 17 us -> 0 us
  Pallas kernels: 55.2 us -> 68.3 us
  local copies, waits for them, and re-layouts: 23.3 us -> 12.6 us
  other arithmetic: 3.96 us -> 2.1 us
    all_to_all x2 -> x0, starting transfers between devices: 17.4 us -> none  [the longest x1 11.9 us: local(): arrived = lax.all_to_all(slots, 'sess', 0, 0, tiled=True)]
    all_to_all x2 -> x0, waiting for transfers between devices: 17 us -> none  [the longest x1 17 us: local(): arrived = lax.all_to_all(slots, 'sess', 0, 0, tiled=True)]
    pallas_call x4 -> x1, Pallas kernels: 55.2 us -> 68.3 us  [local(): pl.pallas_call(functools.partial(fused_kernel, (heads, blocks, sessions,...]
    ppermute x2 -> x0, starting transfers between devices: 5.74 us -> none  [the longest x1 4.46 us: local(): latter = lax.ppermute(end[:share_heads], 'ctx', [(1, 0)])]
    gather x2 -> x0, local copies, waits for them, and re-layouts: 3.62 us -> none  [the longest x1 1.87 us: local(): back[row_session[:, 0]].reshape(flat)]
    select_n x4 -> x0, other arithmetic: 3.57 us -> none  [the longest x2 2.44 us: local(): slots = jnp.where(named.any(axis=1)[:, None, None], q_rows[place], 0)]
    slice x1 -> x0, local copies, waits for them, and re-layouts: 3.14 us -> none  [local(): latter = lax.ppermute(end[:share_heads], 'ctx', [(1, 0)])]
    another operation x7, local copies, waits for them, and re-layouts: 5.14 us -> 2.29 us  [local(): gains = jnp.stack(factors, axis=-1).reshape(flat_rows, steps + 1)]
  transfers between devices with their start and end apart: 4 -> 0, of which waited for: 1 -> 0; matrix products, arithmetic and copies ran while one was open for 14% -> 0% of each run, Pallas kernels for 22% -> 0%
where the time goes in v2:
time: 84.7 us; the launch traced here: 84.5 us
  Pallas kernels  68.3 us (81%)
  local copies, waits for them, and re-layouts  12.6 us (15%)
  other arithmetic  2.1 us (2%)
  between operations  1.42 us (2%)
    pallas_call x1, Pallas kernels, local(): pl.pallas_call(functools.partial(fused_kernel, (heads, blocks, sessions,...  68.3 us
    unnamed x8, local copies, waits for them, and re-layouts  9.55 us
    another operation x7, local copies, waits for them, and re-layouts, local(): gains = jnp.stack(factors, axis=-1).reshape(flat_rows, steps + 1)  2.29 us

profile of v2, /device:TPU:1, one launch (start us, length us, event | category | flops | bytes accessed | tf_op | source)
XLA Modules:
  0.0 84.5 jit_solution(17835309011938822071)
XLA Ops:
  1.3 1.3 %select_reduce_fusion.place_ref = s32[64]{0:T(128)} fusion(s32[32]{0:T(128)} %bitcast.37), kind=kLoop, calls=%fused_computation.8 | loop fusion | flops 6080 | bytes 384 | tf_op jit(solution)/shard_map/reduce_min | solution.py:309
  2.6 0.7 fusion.5
  3.4 0.2 copy.56
  3.6 0.2 stack.22
  3.8 0.2 copy.59
  4.0 0.1 pad.12.clone
  4.1 0.2 stack.19
  4.3 0.2 copy.60
  4.5 0.1 pad.13.clone
  4.7 0.2 stack.20
  4.8 0.2 copy.61
  5.1 0.1 pad.14.clone
  5.2 0.2 stack.21
  5.4 0.2 copy.52
  5.6 0.2 stack.18
  5.8 0.1 stack.23
  5.8 1.8 %copy.48 = f32[1,768,32]{2,1,0:T(8,128)} copy(f32[1,768,32]{1,2,0:T(8,128)} %param.13) | data formatting | bytes 196608 | tf_op args[3]
  7.6 1.3 %copy.57.gains_hbm = f32[2048,5]{1,0:T(8,128)} copy(f32[2048,5]{0,1:T(8,128)S(1)} %stack.23) | data formatting | bytes 81920 | tf_op jit(solution)/shard_map/stack | solution.py:318
  9.0 68.3 %shard_map.113 = (bf16[768,4096]{1,0:T(8,128)(2,1)}, bf16[2048,128]{1,0:T(8,128)(2,1)}) custom-call(s32[1]{0:T(128)S(6)} %copy.64.valid_ref, s32[64]{0:T(128)} %select_reduce_fusion.place_ref, s32[32]{0:T(128)} %bitcast.38, f32[768,32]{1,0:T(8,128)} %bitcast.32, bf16[768,4096]{1,0:T(8,128)(2,1)} %bitcast.29, bf16[768,4096]{1,0:T(8,128)(2,1)} %bitcast.30, ...), custom_call_target="tpu_custom_call" | custom-call | tf_op jit(solution)/shard_map/pallas_call | solution.py:325
  77.3 0.0 copy-start
  77.3 6.3 %copy.65 = bf16[1,768,4096]{2,1,0:T(8,128)(2,1)} copy(bf16[1,768,4096]{2,1,0:T(8,128)(2,1)} %bitcast.28) | data formatting | bytes 12582912
  83.7 0.0 copy-done
  83.7 0.8 copy.66
  (3 shorter events, 0.0 us)
Async XLA Ops:
  77.3 6.4 %copy-start = (bf16[2048,128]{1,0:T(8,128)(2,1)S(1)}, bf16[2048,128]{1,0:T(8,128)(2,1)}, u32[]{:S(2)}) copy-start(bf16[2048,128]{1,0:T(8,128)(2,1)} %get-tuple-element.5) | copy-start | bytes 1572868

commit v3 on v2

v3 whole, which is shorter than its diff:
```python
import functools
import math

import jax
import jax.numpy as jnp
from jax import lax
from jax.experimental import pallas as pl
from jax.experimental.pallas import tpu as pltpu
from jax.sharding import PartitionSpec as P

BLK = 256
DH = 128
SUB = 64
EPSILON = 1e-06
F32 = jnp.float32
BF16 = jnp.bfloat16
MESH = pl.DeviceIdType.MESH
LN2 = math.log(2.0)
EARLY = 8


def dot(a, b, dims=((1,), (0,))):
    return lax.dot_general(a, b, (dims, ((), ())), preferred_element_type=F32)


def iota(shape, axis):
    return lax.broadcasted_iota(jnp.int32, shape, axis)


def split3(value):
    first = value.astype(BF16)
    second = (value - first.astype(F32)).astype(BF16)
    third = (value - first.astype(F32) - second.astype(F32)).astype(BF16)
    return first, second, third


def fused_kernel(
    sizes,
    valid_ref, place_ref, session_ref, rates_ref, step_rates_ref, q_hbm, k_hbm, v_hbm, sq_hbm, sk_hbm, sv_hbm,
    out_ref, decoded_ref,
    qb, kb, vb, sq, sk, sv, slots, arrived, projected, back, recent, carry_gain, gain_table,
    states, other_states, decays, other_decays,
    key_gain, block_gain, entry_gain, row_gain, query_gain, floor, mixed, raw,
    load_sem, step_sem, send_sem, recv_sem, pair_send_sem, pair_recv_sem,
):
    heads, blocks, sessions, rows_here, steps, (side_z, side_y, side_x) = sizes
    share = heads // 2
    groups = heads // 4
    subs = BLK // SUB
    core = lax.axis_index("ctx")
    me = lax.axis_index("sess")
    my_x, my_y, my_z = lax.rem(me, side_x), lax.rem(lax.div(me, side_x), side_y), lax.div(me, side_x * side_y)

    xs = [lax.rem(my_x + d, side_x) for d in range(side_x)]
    ys = [lax.rem(my_y + d, side_y) * side_x for d in range(side_y)]
    zs = [lax.rem(my_z + d, side_z) * (side_x * side_y) for d in range(side_z)]
    peers = [pz + py + px for pz in zs for py in ys for px in xs][1:]

    def block_rows(j):
        return pl.ds(pl.multiple_of(j * BLK, BLK), BLK)

    def load(which, hbm, buffer, j):
        return pltpu.make_async_copy(hbm.at[block_rows(j)], buffer.at[block_rows(j)], load_sem.at[which, j])

    small = [
        pltpu.make_async_copy(a, b, step_sem.at[i])
        for i, (a, b) in enumerate(((sq_hbm, sq), (sk_hbm, sk), (sv_hbm, sv)))
    ]
    small[0].start()
    for j in range(blocks):
        load(0, k_hbm, kb, j).start()
        load(1, v_hbm, vb, j).start()
    for copy in small[1:]:
        copy.start()
    for j in range(blocks):
        load(2, q_hbm, qb, j).start()

    barrier = pltpu.get_barrier_semaphore()
    pl.semaphore_signal(barrier, inc=1, device_id=(1 - core, me), device_id_type=MESH)

    for other in peers:
        pl.semaphore_signal(barrier, inc=1, device_id=(core, other), device_id_type=MESH)

    small[0].wait()

    def fill(s, carry):
        row = place_ref[s]
        slots[s] = jnp.where(row < rows_here, sq[jnp.minimum(row, rows_here - 1)], jnp.zeros(sq.shape[1:], BF16))
        return carry

    lax.fori_loop(0, sessions, fill, 0)
    arrived[me] = slots[me]

    lives = [(core * blocks + j < valid_ref[0]).astype(F32) for j in range(blocks)]
    masked = jnp.concatenate([rates_ref[:, j * BLK:(j + 1) * BLK] * lives[j] for j in range(blocks)], axis=0)
    upper = (iota((BLK, BLK), 0) <= iota((BLK, BLK), 1)).astype(F32).astype(BF16)
    summed = dot(jnp.concatenate(split3(masked), axis=0), upper)
    count = blocks * heads
    running_all = summed[:count] + summed[count:2 * count] + summed[2 * count:]
    lane = iota((heads, BLK), 1)
    passed = jnp.zeros((heads, 1), F32)
    for j in range(blocks):
        running = running_all[j * heads:(j + 1) * heads]
        last = running[:, BLK - 1:BLK]
        key_gain[j] = jnp.exp(running - last) * lives[j]
        block_gain[j] = jnp.broadcast_to(jnp.exp(-last), (heads, DH))
        entry_gain[j] = jnp.broadcast_to(jnp.exp(-passed), (heads, DH))
        passed = passed + last
        centre = None
        for b in range(subs):
            middle = running[:, b * SUB + SUB // 2:b * SUB + SUB // 2 + 1]
            doublings = jnp.round(middle * (1.0 / LN2))
            level = doublings * LN2
            row_gain[j, b] = jnp.exp(running - level)
            query_gain[j, b] = jnp.broadcast_to(jnp.exp2(-doublings), (heads, DH)).astype(BF16).astype(F32)
            centre = level if b == 0 else jnp.where(lane >= b * SUB, level, centre)
        low = (DH * EPSILON) * jnp.exp(2.0 * (running - centre))
        floor[j] = jnp.concatenate([low, jnp.zeros((DH - heads, BLK), F32)], axis=0).T
    for h in range(heads):
        decays[h] = jnp.broadcast_to(entry_gain[blocks - 1, h:h + 1, :] * block_gain[blocks - 1, h:h + 1, :], (8, DH))
    states[0] = jnp.zeros(states.shape[1:], F32)

    per_step = [step_rates_ref[i].astype(F32) for i in range(steps)]
    spans = []
    for delta in range(1, steps + 1):
        spans.append([sum(per_step[max(0, i - delta + 1):i + 1]) for i in range(steps)])
    tables = [
        jnp.concatenate([jnp.exp(-spans[delta - 1][i]) if i >= delta else jnp.zeros_like(per_step[0]) for i in range(steps)], axis=0)
        for delta in range(1, steps)
    ]
    tables.append(jnp.concatenate([jnp.exp(-spans[i][i]) for i in range(steps)], axis=0))
    flat = share * steps
    line = iota((flat, 2 * flat), 0)
    column = lax.rem(iota((flat, 2 * flat), 1), flat)
    pick = (column == lax.rem(line, steps) * share + lax.div(line, steps)).astype(F32).astype(BF16)
    for n, table in enumerate(tables):
        top = table.astype(BF16)
        rest = (table - top.astype(F32)).astype(BF16)
        gain_table[n] = dot(pick, jnp.concatenate([top, rest], axis=0))

    pl.semaphore_wait(barrier, sessions)

    def dispatch(other):
        return pltpu.make_async_remote_copy(
            src_ref=slots.at[other], dst_ref=arrived.at[me], send_sem=send_sem.at[0], recv_sem=recv_sem.at[0],
            device_id=(core, other), device_id_type=MESH)

    def give_back(other):
        return pltpu.make_async_remote_copy(
            src_ref=projected.at[other], dst_ref=back.at[me], send_sem=send_sem.at[1], recv_sem=recv_sem.at[1],
            device_id=(core, other), device_id_type=MESH)

    def wait_all(src, dst, n):
        whole = pltpu.make_async_remote_copy(
            src_ref=src.at[pl.ds(0, sessions - 1)], dst_ref=dst.at[pl.ds(0, sessions - 1)], send_sem=send_sem.at[n],
            recv_sem=recv_sem.at[n], device_id=(core, peers[0]), device_id_type=MESH)
        whole.wait()

    for other in peers:
        dispatch(other).start()

    def group_cols(g):
        return pl.ds(pl.multiple_of(g * 4 * DH, 4 * DH), 4 * DH)

    def state_block(j, carry):
        load(0, k_hbm, kb, j).wait()
        load(1, v_hbm, vb, j).wait()

        def state_group(g, carry):
            rows, cols = block_rows(j), group_cols(g)
            keys, values = kb[rows, cols], vb[rows, cols]
            for one in range(4):
                h = g * 4 + one
                lanes = slice(one * DH, (one + 1) * DH)
                weighted = (keys[:, lanes].T.astype(F32) * key_gain[j, pl.ds(h, 1), :]).astype(BF16)
                states[j + 1, h] = block_gain[j, pl.ds(h, 1), :] * states[j, h] + dot(weighted, values[:, lanes])
            return carry

        return lax.fori_loop(0, groups, state_group, carry)

    lax.fori_loop(0, blocks, state_block, 0)

    theirs, ours = pl.multiple_of((1 - core) * share, share), pl.multiple_of(core * share, share)
    exchange = [
        pltpu.make_async_remote_copy(
            src_ref=a, dst_ref=b, send_sem=pair_send_sem.at[i], recv_sem=pair_recv_sem.at[i],
            device_id=(1 - core, me), device_id_type=MESH)
        for i, (a, b) in enumerate((
            (decays, other_decays),
            (states.at[blocks, pl.ds(theirs, share)], other_states.at[pl.ds(theirs, share)]),
            (states.at[blocks, pl.ds(ours, share)], other_states.at[pl.ds(ours, share)]),
        ))
    ]
    for copy in exchange:
        copy.start()

    for copy in small[1:]:
        copy.wait()
    part = 4 * flat

    def part_rows(p):
        return pl.ds(pl.multiple_of(p * part, part), part)

    def recent_part(p, carry):
        q, k, v = (ref[pl.ds(p * 4, 4)].reshape(part, DH).astype(F32) for ref in (sq, sk, sv))
        own = iota((part, rows_here), 1) == lax.div(iota((part, rows_here), 0), flat) + p * 4

        def gain(n):
            tiled = jnp.concatenate([gain_table[n]] * 4, axis=0)
            return jnp.sum(jnp.where(own, tiled, 0.0), axis=1, keepdims=True)

        total = jnp.sum(q * k, axis=1, keepdims=True) * v
        for delta in range(1, steps):
            affinity = jnp.sum(q * pltpu.roll(k, delta, 0), axis=1, keepdims=True)
            total = total + (affinity * gain(delta - 1)) * pltpu.roll(v, delta, 0)
        recent[part_rows(p), :] = total
        carry_gain[part_rows(p), :] = jnp.broadcast_to(gain(steps - 1), (part, DH))
        return carry

    lax.fori_loop(0, rows_here // 4, recent_part, 0)

    for copy in exchange:
        copy.wait()

    half = BLK // 2
    first_core = core == 0
    per_half = half // SUB

    laps = blocks * groups
    live = [(core * blocks + j < valid_ref[0]).astype(F32) * math.sqrt(DH) for j in range(blocks)]

    def place_of(lap):
        lap = jnp.clip(lap, 0, laps - 1)
        return lax.div(lap, groups), lax.rem(lap, groups)

    def start_scores(lap):
        j, g = place_of(lap)
        rows, cols = block_rows(j), group_cols(g)
        q4, k4 = qb[rows, cols], kb[rows, cols]
        for one in range(4):
            h = g * 4 + one
            lanes = slice(one * DH, (one + 1) * DH)
            q, k = q4[:, lanes], k4[:, lanes]
            for side in range(2):
                here = slice(side * half, (side + 1) * half)
                seen = (side + 1) * half
                scores = dot(q[here], k[:seen], ((1,), (1,)))
                pieces = []
                for b in range(per_half):
                    n = side * per_half + b
                    piece = scores[b * SUB:(b + 1) * SUB] * row_gain[j, n, pl.ds(h, 1), :][:, :seen]
                    causal = iota((SUB, half), 0) + b * SUB >= iota((SUB, half), 1)
                    latest = jnp.where(causal, piece[:, seen - half:], 0.0)
                    scaled = q[here][b * SUB:(b + 1) * SUB].astype(F32) * query_gain[j, n, pl.ds(h, 1), :]
                    pieces.append(jnp.concatenate(([piece[:, :half]] if side else []) + [latest, scaled], axis=1).astype(BF16))
                mixed[one, :, side * 2 * half:side * 2 * half + seen + half] = jnp.concatenate(pieces, axis=0)

    def apply_values(lap):
        j, g = place_of(lap)
        v4 = vb[block_rows(j), group_cols(g)]
        for one in range(4):
            h = g * 4 + one
            v = v4[:, one * DH:(one + 1) * DH]
            prefix = jnp.where(first_core, 0.0, entry_gain[j, pl.ds(h, 1), :] * other_states[h])
            entering = (prefix + states[j, h]).astype(BF16)
            for side in range(2):
                seen = (side + 1) * half
                weights = mixed[one, :, side * 2 * half:side * 2 * half + seen + half]
                raw[one, side * half:(side + 1) * half, :] = dot(weights, jnp.concatenate([v[:seen], entering], axis=0))

    def normalize(lap):
        j, g = place_of(lap)
        alive = jnp.where(j == 0, live[0], live[1])
        for n in range(2, blocks):
            alive = jnp.where(j == n, live[n], alive)
        for one in range(4):
            h = g * 4 + one
            for side in range(2):
                here = slice(side * half, (side + 1) * half)
                mix = raw[one, here, :]
                low = jnp.where(iota((half, DH), 1) == h, floor[j, here, :], 0.0)
                scale = lax.rsqrt(jnp.sum(mix * mix + low, axis=1, keepdims=True)) * alive
                out_ref[pl.ds(pl.multiple_of(j * BLK + side * half, half), half), pl.ds(pl.multiple_of(h * DH, DH), DH)] = (
                    mix * scale).astype(BF16)

    def output_lap(lap, carry):
        normalize(lap - 2)
        apply_values(lap - 1)
        start_scores(lap)
        return carry

    for j in range(blocks):
        load(2, q_hbm, qb, j).wait()
    raw[...] = jnp.zeros(raw.shape, F32)
    mixed[...] = jnp.zeros(mixed.shape, BF16)
    lax.fori_loop(0, EARLY, output_lap, 0)

    wait_all(slots, arrived, 0)

    def project(quad, carry):
        place = pl.ds(pl.multiple_of(quad * 16, 16), 16)
        x = arrived[:, place, :].reshape(sessions * 16, DH)
        doubled = jnp.concatenate([x, x], axis=1)
        position = lax.div(lax.rem(iota((sessions * 16, DH), 0), 16), 4)
        chosen = None
        for two in range(2):
            columns = []
            for one in range(2):
                h = core * share + quad * 4 + two * 2 + one
                mine, other = states[blocks, h], other_states[h]
                earlier = jnp.where(first_core, mine, other)
                latter = jnp.where(first_core, other, mine)
                decay = jnp.where(first_core, other_decays[h, 0:1, :], decays[h, 0:1, :])
                final = decay * earlier + latter
                top = final.astype(BF16)
                rest = (final - top.astype(F32)).astype(BF16)
                columns.append(jnp.concatenate([top, rest], axis=0))
            product = dot(doubled, jnp.concatenate(columns, axis=1))
            for one in range(2):
                piece = product[:, one * DH:(one + 1) * DH]
                chosen = piece if chosen is None else jnp.where(position == two * 2 + one, piece, chosen)
        projected[:, place, :] = chosen.astype(BF16).reshape(sessions, 16, DH)
        return carry

    lax.fori_loop(0, share // 4, project, 0)
    back[me] = projected[me]
    for other in peers:
        give_back(other).start()

    lax.fori_loop(EARLY, laps + 2, output_lap, 0)

    wait_all(projected, back, 1)

    def finish(p, carry):
        rows = part_rows(p)
        pieces = [back[session_ref[p * 4 + i]].astype(F32) for i in range(4)]
        reading = carry_gain[rows, :] * jnp.concatenate(pieces, axis=0) + recent[rows, :]
        scale = lax.rsqrt(jnp.mean(reading * reading, axis=1, keepdims=True) + EPSILON)
        decoded_ref[rows, :] = (reading * scale).astype(BF16)
        return carry

    lax.fori_loop(0, rows_here // 4, finish, 0)


def local(side, query_rows, key_rows, value_rows, decay_rates, valid_blocks, step_queries, step_keys, step_values, step_rates, row_session):
    tokens, width = query_rows.shape[1:]
    heads = decay_rates.shape[2]
    blocks = tokens // BLK
    subs = BLK // SUB
    row_count, steps, share_width = step_queries.shape
    share = share_width // DH
    sessions = lax.axis_size("sess")

    def by_head(data):
        return data.reshape(row_count, steps, share, DH).transpose(0, 2, 1, 3).reshape(row_count, share * steps, DH)

    named = row_session[:, 0][None, :] == jnp.arange(sessions, dtype=jnp.int32)[:, None]
    place = jnp.min(jnp.where(named, jnp.arange(row_count, dtype=jnp.int32)[None, :], row_count), axis=1)
    flat_rows = row_count * share * steps

    smem = pl.BlockSpec(memory_space=pltpu.SMEM)
    vmem = pl.BlockSpec(memory_space=pltpu.VMEM)
    hbm = pl.BlockSpec(memory_space=pl.ANY)
    slot = (share * steps, DH)
    dma = pltpu.SemaphoreType.DMA
    prefill_out, decoded = pl.pallas_call(
        functools.partial(fused_kernel, (heads, blocks, sessions, row_count, steps, side)),
        out_shape=(pltpu.VMEM((tokens, width), BF16), jax.ShapeDtypeStruct((flat_rows, DH), BF16)),
        in_specs=[smem, smem, smem, vmem, vmem] + [hbm] * 6,
        out_specs=(vmem, vmem),
        scratch_shapes=[
            pltpu.VMEM((tokens, width), BF16), pltpu.VMEM((tokens, width), BF16), pltpu.VMEM((tokens, width), BF16),
            pltpu.VMEM((row_count,) + slot, BF16), pltpu.VMEM((row_count,) + slot, BF16), pltpu.VMEM((row_count,) + slot, BF16),
            pltpu.VMEM((sessions,) + slot, BF16), pltpu.VMEM((sessions,) + slot, BF16),
            pltpu.VMEM((sessions,) + slot, BF16), pltpu.VMEM((sessions,) + slot, BF16),
            pltpu.VMEM((flat_rows, DH), F32), pltpu.VMEM((flat_rows, DH), F32), pltpu.VMEM((steps, share * steps, row_count), F32),
            pltpu.VMEM((blocks + 1, heads, DH, DH), F32), pltpu.VMEM((heads, DH, DH), F32),
            pltpu.VMEM((heads, 8, DH), F32), pltpu.VMEM((heads, 8, DH), F32),
            pltpu.VMEM((blocks, heads, BLK), F32), pltpu.VMEM((blocks, heads, DH), F32), pltpu.VMEM((blocks, heads, DH), F32),
            pltpu.VMEM((blocks, subs, heads, BLK), F32), pltpu.VMEM((blocks, subs, heads, DH), F32),
            pltpu.VMEM((blocks, BLK, DH), F32), pltpu.VMEM((4, BLK // 2, 5 * BLK // 2), BF16), pltpu.VMEM((4, BLK, DH), F32),
            dma((3, blocks)), dma((3,)), dma((2,)), dma((2,)), dma((3,)), dma((3,)),
        ],
        compiler_params=pltpu.CompilerParams(collective_id=0, has_side_effects=True, vmem_limit_bytes=48 << 20),
    )(valid_blocks, place, row_session[:, 0], decay_rates[0].T, step_rates.transpose(1, 2, 0), query_rows[0], key_rows[0], value_rows[0],
      by_head(step_queries), by_head(step_keys), by_head(step_values))
    decode_out = decoded.reshape(row_count, share, steps, DH).transpose(0, 2, 1, 3).reshape(row_count, steps, share_width)
    return prefill_out[None], decode_out


def solution(mesh):
    long, step = P("sess", "ctx", None), P("sess", None, "ctx")
    devices = mesh.shape["sess"]
    side = round(devices ** (1 / 3))
    sides = (side, side, side) if side ** 3 == devices else (1, 1, devices)
    return jax.shard_map(
        functools.partial(local, sides),
        mesh=mesh,
        in_specs=(long, long, long, long, P("sess"), step, step, step, step, P("sess", None)),
        out_specs=(long, step),
        check_vma=False,
    )
```

time: 84.7 us -> 53.9 us (0.64)
  Pallas kernels: 68.3 us -> 47.4 us
  local copies, waits for them, and re-layouts: 12.6 us -> 3.5 us
  other arithmetic: 2.1 us -> 1.25 us
    pallas_call x1, Pallas kernels: 68.3 us -> 47.4 us  [local(): pl.pallas_call(functools.partial(fused_kernel, (heads, blocks, sessions,...]
    unnamed x8 -> x4, local copies, waits for them, and re-layouts: 9.55 us -> 3.5 us
    another operation x7 -> x0, local copies, waits for them, and re-layouts: 2.29 us -> none  [local(): gains = jnp.stack(factors, axis=-1).reshape(flat_rows, steps + 1)]
where the time goes in v3:
time: 53.9 us; the launch traced here: 53.5 us
  Pallas kernels  47.4 us (88%)
  local copies, waits for them, and re-layouts  3.5 us (6%)
  between operations  1.29 us (2%)
  other arithmetic  1.25 us (2%)
    pallas_call x1, Pallas kernels, local(): pl.pallas_call(functools.partial(fused_kernel, (heads, blocks, sessions,...  47.4 us
    unnamed x4, local copies, waits for them, and re-layouts  3.5 us
    reduce_min x1, other arithmetic, local(): jnp.min(jnp.where(named, jnp.arange(row_count, dtype=jnp.int32)[None, :],...  1.25 us

profile of v3, /device:TPU:1, one launch (start us, length us, event | category | flops | bytes accessed | tf_op | source)
XLA Modules:
  0.0 53.5 jit_solution(18352640816149626302)
XLA Ops:
  1.3 1.3 %select_reduce_fusion.place_ref = s32[64]{0:T(128)} fusion(s32[32]{0:T(128)} %bitcast.39), kind=kLoop, calls=%fused_computation | loop fusion | flops 6080 | bytes 384 | tf_op jit(solution)/shard_map/reduce_min | solution.py:358
  2.5 47.4 %shard_map.113 = (bf16[768,4096]{1,0:T(8,128)(2,1)S(1)}, bf16[2048,128]{1,0:T(8,128)(2,1)}) custom-call(s32[1]{0:T(128)S(6)} %copy.23.valid_ref, s32[64]{0:T(128)} %select_reduce_fusion.place_ref, s32[32]{0:T(128)} %bitcast.40, f32[32,768]{1,0:T(8,128)} %bitcast.37, bf16[4,16,32]{2,1,0:T(8,128)(2,1)} %bitcast.38, bf16[768,4096]{1,0:T(8,128)(2,1)} %bitcast.30, ...), custom_call_target="tpu_custom_call" | custom-call | tf_op jit(solution)/shard_map/pallas_call | solution.py:366
  49.9 0.0 copy-start
  50.0 2.7 %copy.22 = bf16[1,768,4096]{2,1,0:T(8,128)(2,1)} copy(bf16[1,768,4096]{2,1,0:T(8,128)(2,1)S(1)} %bitcast.29) | data formatting | bytes 12582912
  52.7 0.0 copy-done
  52.7 0.8 %copy.24 = bf16[32,4,2048]{2,1,0:T(4,128)(2,1)} copy(bf16[32,4,2048]{2,1,0:T(4,128)(2,1)S(1)} %bitcast.33) | data formatting | bytes 1048576
Async XLA Ops:
  49.9 2.7 %copy-start = (bf16[2048,128]{1,0:T(8,128)(2,1)S(1)}, bf16[2048,128]{1,0:T(8,128)(2,1)}, u32[]{:S(2)}) copy-start(bf16[2048,128]{1,0:T(8,128)(2,1)} %get-tuple-element.5) | copy-start | bytes 1572868

commit v4 on v3

--- a/solution.py
+++ b/solution.py
@@ -16,7 +16,7 @@
 BF16 = jnp.bfloat16
 MESH = pl.DeviceIdType.MESH
 LN2 = math.log(2.0)
-EARLY = 8
+EARLY = 4
 
 
 def dot(a, b, dims=((1,), (0,))):
@@ -34,11 +34,34 @@
     return first, second, third
 
 
+def far_first(side_x, side_y, side_z):
+    sides = (side_x, side_y, side_z)
+
+    def hops(offset):
+        return sum(min(d, n - d) for d, n in zip(offset, sides))
+
+    def orbit(offset):
+        turned = [offset]
+        if side_x == side_y == side_z:
+            turned += [offset[1:] + offset[:1], offset[2:] + offset[:2]]
+        for one in turned:
+            yield one
+            yield tuple((n - d) % n for d, n in zip(one, sides))
+
+    every = [(a, b, c) for a in range(side_x) for b in range(side_y) for c in range(side_z)][1:]
+    order = []
+    for offset in sorted(every, key=lambda o: (-hops(o), o)):
+        for one in orbit(offset):
+            if one not in order:
+                order.append(one)
+    return order
+
+
 def fused_kernel(
     sizes,
-    valid_ref, place_ref, session_ref, rates_ref, step_rates_ref, q_hbm, k_hbm, v_hbm, sq_hbm, sk_hbm, sv_hbm,
+    valid_ref, place_ref, session_ref, rates_hbm, step_rates_hbm, q_hbm, k_hbm, v_hbm, sq_hbm, sk_hbm, sv_hbm,
     out_ref, decoded_ref,
-    qb, kb, vb, sq, sk, sv, slots, arrived, projected, back, recent, carry_gain, gain_table,
+    qb, kb, vb, rates_ref, step_rates_ref, sq, sk, sv, slots, arrived, projected, back, recent, carry_gain, gain_table,
     states, other_states, decays, other_decays,
     key_gain, block_gain, entry_gain, row_gain, query_gain, floor, mixed, raw,
     load_sem, step_sem, send_sem, recv_sem, pair_send_sem, pair_recv_sem,
@@ -54,7 +77,7 @@
     xs = [lax.rem(my_x + d, side_x) for d in range(side_x)]
     ys = [lax.rem(my_y + d, side_y) * side_x for d in range(side_y)]
     zs = [lax.rem(my_z + d, side_z) * (side_x * side_y) for d in range(side_z)]
-    peers = [pz + py + px for pz in zs for py in ys for px in xs][1:]
+    peers = [zs[c] + ys[b] + xs[a] for a, b, c in far_first(side_x, side_y, side_z)]
 
     def block_rows(j):
         return pl.ds(pl.multiple_of(j * BLK, BLK), BLK)
@@ -64,13 +87,14 @@
 
     small = [
         pltpu.make_async_copy(a, b, step_sem.at[i])
-        for i, (a, b) in enumerate(((sq_hbm, sq), (sk_hbm, sk), (sv_hbm, sv)))
+        for i, (a, b) in enumerate(((sq_hbm, sq), (rates_hbm, rates_ref), (step_rates_hbm, step_rates_ref), (sk_hbm, sk), (sv_hbm, sv)))
     ]
-    small[0].start()
+    for copy in small[:3]:
+        copy.start()
     for j in range(blocks):
         load(0, k_hbm, kb, j).start()
         load(1, v_hbm, vb, j).start()
-    for copy in small[1:]:
+    for copy in small[3:]:
         copy.start()
     for j in range(blocks):
         load(2, q_hbm, qb, j).start()
@@ -91,6 +115,8 @@
     lax.fori_loop(0, sessions, fill, 0)
     arrived[me] = slots[me]
 
+    for copy in small[1:3]:
+        copy.wait()
     lives = [(core * blocks + j < valid_ref[0]).astype(F32) for j in range(blocks)]
     masked = jnp.concatenate([rates_ref[:, j * BLK:(j + 1) * BLK] * lives[j] for j in range(blocks)], axis=0)
     upper = (iota((BLK, BLK), 0) <= iota((BLK, BLK), 1)).astype(F32).astype(BF16)
@@ -194,7 +220,7 @@
     for copy in exchange:
         copy.start()
 
-    for copy in small[1:]:
+    for copy in small[3:]:
         copy.wait()
     part = 4 * flat
 
@@ -301,7 +327,7 @@
         place = pl.ds(pl.multiple_of(quad * 16, 16), 16)
         x = arrived[:, place, :].reshape(sessions * 16, DH)
         doubled = jnp.concatenate([x, x], axis=1)
-        position = lax.div(lax.rem(iota((sessions * 16, DH), 0), 16), 4)
+        position = lax.div(iota((1, 16, DH), 1), 4)
         chosen = None
         for two in range(2):
             columns = []
@@ -317,9 +343,9 @@
                 columns.append(jnp.concatenate([top, rest], axis=0))
             product = dot(doubled, jnp.concatenate(columns, axis=1))
             for one in range(2):
-                piece = product[:, one * DH:(one + 1) * DH]
+                piece = product[:, one * DH:(one + 1) * DH].reshape(sessions, 16, DH)
                 chosen = piece if chosen is None else jnp.where(position == two * 2 + one, piece, chosen)
-        projected[:, place, :] = chosen.astype(BF16).reshape(sessions, 16, DH)
+        projected[:, place, :] = chosen.astype(BF16)
         return carry
 
     lax.fori_loop(0, share // 4, project, 0)
@@ -365,11 +391,12 @@
     dma = pltpu.SemaphoreType.DMA
     prefill_out, decoded = pl.pallas_call(
         functools.partial(fused_kernel, (heads, blocks, sessions, row_count, steps, side)),
-        out_shape=(pltpu.VMEM((tokens, width), BF16), jax.ShapeDtypeStruct((flat_rows, DH), BF16)),
-        in_specs=[smem, smem, smem, vmem, vmem] + [hbm] * 6,
+        out_shape=(pltpu.VMEM((tokens, width), BF16), pltpu.VMEM((flat_rows, DH), BF16)),
+        in_specs=[smem, smem, smem] + [hbm] * 8,
         out_specs=(vmem, vmem),
         scratch_shapes=[
             pltpu.VMEM((tokens, width), BF16), pltpu.VMEM((tokens, width), BF16), pltpu.VMEM((tokens, width), BF16),
+            pltpu.VMEM((heads, tokens), F32), pltpu.VMEM((steps, share, row_count), BF16),
             pltpu.VMEM((row_count,) + slot, BF16), pltpu.VMEM((row_count,) + slot, BF16), pltpu.VMEM((row_count,) + slot, BF16),
             pltpu.VMEM((sessions,) + slot, BF16), pltpu.VMEM((sessions,) + slot, BF16),
             pltpu.VMEM((sessions,) + slot, BF16), pltpu.VMEM((sessions,) + slot, BF16),
@@ -379,7 +406,7 @@
             pltpu.VMEM((blocks, heads, BLK), F32), pltpu.VMEM((blocks, heads, DH), F32), pltpu.VMEM((blocks, heads, DH), F32),
             pltpu.VMEM((blocks, subs, heads, BLK), F32), pltpu.VMEM((blocks, subs, heads, DH), F32),
             pltpu.VMEM((blocks, BLK, DH), F32), pltpu.VMEM((4, BLK // 2, 5 * BLK // 2), BF16), pltpu.VMEM((4, BLK, DH), F32),
-            dma((3, blocks)), dma((3,)), dma((2,)), dma((2,)), dma((3,)), dma((3,)),
+            dma((3, blocks)), dma((5,)), dma((2,)), dma((2,)), dma((3,)), dma((3,)),
         ],
         compiler_params=pltpu.CompilerParams(collective_id=0, has_side_effects=True, vmem_limit_bytes=48 << 20),
     )(valid_blocks, place, row_session[:, 0], decay_rates[0].T, step_rates.transpose(1, 2, 0), query_rows[0], key_rows[0], value_rows[0],

time: 53.9 us -> 48.5 us (0.90)
  Pallas kernels: 47.4 us -> 42.4 us
    pallas_call x1, Pallas kernels: 47.4 us -> 42.4 us  [local(): pl.pallas_call(functools.partial(fused_kernel, (heads, blocks, sessions,...]
    unnamed x4 -> x2, local copies, waits for them, and re-layouts: 3.5 us -> 3.5 us
where the time goes in v4:
time: 48.5 us; the launch traced here: 48.4 us
  Pallas kernels  42.4 us (87%)
  local copies, waits for them, and re-layouts  3.5 us (7%)
  between operations  1.29 us (3%)
  other arithmetic  1.25 us (3%)
    pallas_call x1, Pallas kernels, local(): pl.pallas_call(functools.partial(fused_kernel, (heads, blocks, sessions,...  42.4 us
    unnamed x2, local copies, waits for them, and re-layouts  3.5 us
    reduce_min x1, other arithmetic, local(): jnp.min(jnp.where(named, jnp.arange(row_count, dtype=jnp.int32)[None, :],...  1.25 us

profile of v4, /device:TPU:1, one launch (start us, length us, event | category | flops | bytes accessed | tf_op | source)
XLA Modules:
  0.0 48.4 jit_solution(15175177948246532475)
XLA Ops:
  1.3 1.3 %select_reduce_fusion.place_ref = s32[64]{0:T(128)} fusion(s32[32]{0:T(128)} %bitcast.39), kind=kLoop, calls=%fused_computation | loop fusion | flops 6080 | bytes 384 | tf_op jit(solution)/shard_map/reduce_min | solution.py:384
  2.5 42.4 %shard_map.113 = (bf16[768,4096]{1,0:T(8,128)(2,1)S(1)}, bf16[2048,128]{1,0:T(8,128)(2,1)S(1)}) custom-call(s32[1]{0:T(128)S(6)} %copy.24.valid_ref, s32[64]{0:T(128)} %select_reduce_fusion.place_ref, s32[32]{0:T(128)} %bitcast.40, f32[32,768]{1,0:T(8,128)} %bitcast.37, bf16[4,16,32]{2,1,0:T(8,128)(2,1)} %bitcast.38, bf16[768,4096]{1,0:T(8,128)(2,1)} %bitcast.31, ...), custom_call_target="tpu_custom_call" | custom-call | tf_op jit(solution)/shard_map/pallas_call | solution.py:392
  44.9 2.7 %copy.22 = bf16[1,768,4096]{2,1,0:T(8,128)(2,1)} copy(bf16[1,768,4096]{2,1,0:T(8,128)(2,1)S(1)} %bitcast.29) | data formatting | bytes 12582912
  47.6 0.8 %copy.23 = bf16[32,4,2048]{2,1,0:T(4,128)(2,1)} copy(bf16[32,4,2048]{2,1,0:T(4,128)(2,1)S(1)} %bitcast.30) | data formatting | bytes 1048576

commit v5 on v4

--- a/solution.py
+++ b/solution.py
@@ -16,7 +16,7 @@
 BF16 = jnp.bfloat16
 MESH = pl.DeviceIdType.MESH
 LN2 = math.log(2.0)
-EARLY = 4
+EARLY = 3
 
 
 def dot(a, b, dims=((1,), (0,))):
@@ -77,7 +77,9 @@
     xs = [lax.rem(my_x + d, side_x) for d in range(side_x)]
     ys = [lax.rem(my_y + d, side_y) * side_x for d in range(side_y)]
     zs = [lax.rem(my_z + d, side_z) * (side_x * side_y) for d in range(side_z)]
-    peers = [zs[c] + ys[b] + xs[a] for a, b, c in far_first(side_x, side_y, side_z)]
+    order = far_first(side_x, side_y, side_z)
+    peers = [zs[c] + ys[b] + xs[a] for a, b, c in order]
+    origins = [zs[-c] + ys[-b] + xs[-a] for a, b, c in order]
 
     def block_rows(j):
         return pl.ds(pl.multiple_of(j * BLK, BLK), BLK)
@@ -113,7 +115,33 @@
         return carry
 
     lax.fori_loop(0, sessions, fill, 0)
-    arrived[me] = slots[me]
+    arrived[sessions - 1] = slots[me]
+
+    pl.semaphore_wait(barrier, sessions)
+
+    count_a = sessions // 2
+    peer_spans = ((0, count_a), (count_a, sessions - 1))
+
+    def dispatch(n):
+        group = int(n >= count_a)
+        return pltpu.make_async_remote_copy(
+            src_ref=slots.at[peers[n]], dst_ref=arrived.at[n], send_sem=send_sem.at[group], recv_sem=recv_sem.at[group],
+            device_id=(core, peers[n]), device_id_type=MESH)
+
+    def give_back(n):
+        return pltpu.make_async_remote_copy(
+            src_ref=projected.at[n], dst_ref=back.at[me], send_sem=send_sem.at[2], recv_sem=recv_sem.at[2],
+            device_id=(core, origins[n]), device_id_type=MESH)
+
+    def wait_all(src, dst, span, n):
+        part = pl.ds(span[0], span[1] - span[0])
+        whole = pltpu.make_async_remote_copy(
+            src_ref=src.at[part], dst_ref=dst.at[part], send_sem=send_sem.at[n],
+            recv_sem=recv_sem.at[n], device_id=(core, peers[0]), device_id_type=MESH)
+        whole.wait()
+
+    for n in range(sessions - 1):
+        dispatch(n).start()
 
     for copy in small[1:3]:
         copy.wait()
@@ -164,61 +192,52 @@
         rest = (table - top.astype(F32)).astype(BF16)
         gain_table[n] = dot(pick, jnp.concatenate([top, rest], axis=0))
 
-    pl.semaphore_wait(barrier, sessions)
-
-    def dispatch(other):
-        return pltpu.make_async_remote_copy(
-            src_ref=slots.at[other], dst_ref=arrived.at[me], send_sem=send_sem.at[0], recv_sem=recv_sem.at[0],
-            device_id=(core, other), device_id_type=MESH)
-
-    def give_back(other):
-        return pltpu.make_async_remote_copy(
-            src_ref=projected.at[other], dst_ref=back.at[me], send_sem=send_sem.at[1], recv_sem=recv_sem.at[1],
-            device_id=(core, other), device_id_type=MESH)
-
-    def wait_all(src, dst, n):
-        whole = pltpu.make_async_remote_copy(
-            src_ref=src.at[pl.ds(0, sessions - 1)], dst_ref=dst.at[pl.ds(0, sessions - 1)], send_sem=send_sem.at[n],
-            recv_sem=recv_sem.at[n], device_id=(core, peers[0]), device_id_type=MESH)
-        whole.wait()
-
-    for other in peers:
-        dispatch(other).start()
-
     def group_cols(g):
         return pl.ds(pl.multiple_of(g * 4 * DH, 4 * DH), 4 * DH)
+
+    def state_lap(j, g):
+        rows, cols = block_rows(j), group_cols(g)
+        keys, values = kb[rows, cols], vb[rows, cols]
+        for one in range(4):
+            h = g * 4 + one
+            lanes = slice(one * DH, (one + 1) * DH)
+            weighted = (keys[:, lanes].T.astype(F32) * key_gain[j, pl.ds(h, 1), :]).astype(BF16)
+            states[j + 1, h] = block_gain[j, pl.ds(h, 1), :] * states[j, h] + dot(weighted, values[:, lanes])
 
     def state_block(j, carry):
         load(0, k_hbm, kb, j).wait()
         load(1, v_hbm, vb, j).wait()
 
         def state_group(g, carry):
-            rows, cols = block_rows(j), group_cols(g)
-            keys, values = kb[rows, cols], vb[rows, cols]
-            for one in range(4):
-                h = g * 4 + one
-                lanes = slice(one * DH, (one + 1) * DH)
-                weighted = (keys[:, lanes].T.astype(F32) * key_gain[j, pl.ds(h, 1), :]).astype(BF16)
-                states[j + 1, h] = block_gain[j, pl.ds(h, 1), :] * states[j, h] + dot(weighted, values[:, lanes])
+            state_lap(j, g)
             return carry
 
         return lax.fori_loop(0, groups, state_group, carry)
 
-    lax.fori_loop(0, blocks, state_block, 0)
-
-    theirs, ours = pl.multiple_of((1 - core) * share, share), pl.multiple_of(core * share, share)
-    exchange = [
-        pltpu.make_async_remote_copy(
-            src_ref=a, dst_ref=b, send_sem=pair_send_sem.at[i], recv_sem=pair_recv_sem.at[i],
-            device_id=(1 - core, me), device_id_type=MESH)
-        for i, (a, b) in enumerate((
-            (decays, other_decays),
-            (states.at[blocks, pl.ds(theirs, share)], other_states.at[pl.ds(theirs, share)]),
-            (states.at[blocks, pl.ds(ours, share)], other_states.at[pl.ds(ours, share)]),
-        ))
-    ]
-    for copy in exchange:
-        copy.start()
+    decay_copy = pltpu.make_async_remote_copy(
+        src_ref=decays, dst_ref=other_decays, send_sem=pair_send_sem.at[2], recv_sem=pair_recv_sem.at[2],
+        device_id=(1 - core, me), device_id_type=MESH)
+    decay_copy.start()
+    lax.fori_loop(0, blocks - 1, state_block, 0)
+
+    load(0, k_hbm, kb, blocks - 1).wait()
+    load(1, v_hbm, vb, blocks - 1).wait()
+
+    def send_states(first, n, which):
+        some = pl.ds(first, n)
+        return pltpu.make_async_remote_copy(
+            src_ref=states.at[blocks, some], dst_ref=other_states.at[some], send_sem=pair_send_sem.at[which],
+            recv_sem=pair_recv_sem.at[which], device_id=(1 - core, me), device_id_type=MESH)
+
+    for which in range(2):
+        first = (1 - core if which == 0 else core) * (groups // 2)
+
+        def last_group(g, carry):
+            state_lap(blocks - 1, first + g)
+            send_states((first + g) * 4, 4, which).start()
+            return carry
+
+        lax.fori_loop(0, groups // 2, last_group, 0)
 
     for copy in small[3:]:
         copy.wait()
@@ -244,9 +263,6 @@
         return carry
 
     lax.fori_loop(0, rows_here // 4, recent_part, 0)
-
-    for copy in exchange:
-        copy.wait()
 
     half = BLK // 2
     first_core = core == 0
@@ -315,47 +331,59 @@
         start_scores(lap)
         return carry
 
+    def project_group(low, high):
+        many = high - low
+
+        def project(quad, carry):
+            place = pl.ds(pl.multiple_of(quad * 16, 16), 16)
+            x = arrived[low:high, place, :].reshape(many * 16, DH)
+            doubled = jnp.concatenate([x, x], axis=1)
+            position = lax.div(iota((1, 16, DH), 1), 4)
+            chosen = None
+            for two in range(2):
+                columns = []
+                for one in range(2):
+                    h = core * share + quad * 4 + two * 2 + one
+                    mine, other = states[blocks, h], other_states[h]
+                    earlier = jnp.where(first_core, mine, other)
+                    latter = jnp.where(first_core, other, mine)
+                    decay = jnp.where(first_core, other_decays[h, 0:1, :], decays[h, 0:1, :])
+                    final = decay * earlier + latter
+                    top = final.astype(BF16)
+                    rest = (final - top.astype(F32)).astype(BF16)
+                    columns.append(jnp.concatenate([top, rest], axis=0))
+                product = dot(doubled, jnp.concatenate(columns, axis=1))
+                for one in range(2):
+                    piece = product[:, one * DH:(one + 1) * DH].reshape(many, 16, DH)
+                    chosen = piece if chosen is None else jnp.where(position == two * 2 + one, piece, chosen)
+            projected[low:high, place, :] = chosen.astype(BF16)
+            return carry
+
+        lax.fori_loop(0, share // 4, project, 0)
+
+    raw[...] = jnp.zeros(raw.shape, F32)
+    mixed[...] = jnp.zeros(mixed.shape, BF16)
+    decay_copy.wait()
+    send_states(pl.multiple_of(core * share, share), share, 0).wait()
+    wait_all(slots, arrived, peer_spans[0], 0)
+    project_group(0, count_a)
+    for n in range(count_a):
+        give_back(n).start()
+
     for j in range(blocks):
         load(2, q_hbm, qb, j).wait()
-    raw[...] = jnp.zeros(raw.shape, F32)
-    mixed[...] = jnp.zeros(mixed.shape, BF16)
+    send_states(pl.multiple_of((1 - core) * share, share), share, 1).wait()
     lax.fori_loop(0, EARLY, output_lap, 0)
 
-    wait_all(slots, arrived, 0)
-
-    def project(quad, carry):
-        place = pl.ds(pl.multiple_of(quad * 16, 16), 16)
-        x = arrived[:, place, :].reshape(sessions * 16, DH)
-        doubled = jnp.concatenate([x, x], axis=1)
-        position = lax.div(iota((1, 16, DH), 1), 4)
-        chosen = None
-        for two in range(2):
-            columns = []
-            for one in range(2):
-                h = core * share + quad * 4 + two * 2 + one
-                mine, other = states[blocks, h], other_states[h]
-                earlier = jnp.where(first_core, mine, other)
-                latter = jnp.where(first_core, other, mine)
-                decay = jnp.where(first_core, other_decays[h, 0:1, :], decays[h, 0:1, :])
-                final = decay * earlier + latter
-                top = final.astype(BF16)
-                rest = (final - top.astype(F32)).astype(BF16)
-                columns.append(jnp.concatenate([top, rest], axis=0))
-            product = dot(doubled, jnp.concatenate(columns, axis=1))
-            for one in range(2):
-                piece = product[:, one * DH:(one + 1) * DH].reshape(sessions, 16, DH)
-                chosen = piece if chosen is None else jnp.where(position == two * 2 + one, piece, chosen)
-        projected[:, place, :] = chosen.astype(BF16)
-        return carry
-
-    lax.fori_loop(0, share // 4, project, 0)
-    back[me] = projected[me]
-    for other in peers:
-        give_back(other).start()
+    wait_all(slots, arrived, peer_spans[1], 1)
+    project_group(count_a, sessions)
+    back[me] = projected[sessions - 1]
+    for n in range(count_a, sessions - 1):
+        give_back(n).start()
 
     lax.fori_loop(EARLY, laps + 2, output_lap, 0)
 
-    wait_all(projected, back, 1)
+    wait_all(projected, back, (0, sessions - 1), 2)
 
     def finish(p, carry):
         rows = part_rows(p)
@@ -406,7 +434,7 @@
             pltpu.VMEM((blocks, heads, BLK), F32), pltpu.VMEM((blocks, heads, DH), F32), pltpu.VMEM((blocks, heads, DH), F32),
             pltpu.VMEM((blocks, subs, heads, BLK), F32), pltpu.VMEM((blocks, subs, heads, DH), F32),
             pltpu.VMEM((blocks, BLK, DH), F32), pltpu.VMEM((4, BLK // 2, 5 * BLK // 2), BF16), pltpu.VMEM((4, BLK, DH), F32),
-            dma((3, blocks)), dma((5,)), dma((2,)), dma((2,)), dma((3,)), dma((3,)),
+            dma((3, blocks)), dma((5,)), dma((3,)), dma((3,)), dma((3,)), dma((3,)),
         ],
         compiler_params=pltpu.CompilerParams(collective_id=0, has_side_effects=True, vmem_limit_bytes=48 << 20),
     )(valid_blocks, place, row_session[:, 0], decay_rates[0].T, step_rates.transpose(1, 2, 0), query_rows[0], key_rows[0], value_rows[0],

time: 48.5 us -> 46 us (0.948); the launches traced: 48.4 us -> 45.1 us
  Pallas kernels: 42.4 us -> 39.1 us
    pallas_call x1, Pallas kernels: 42.4 us -> 39.1 us  [local(): pl.pallas_call(functools.partial(fused_kernel, (heads, blocks, sessions,...]
where the time goes in v5:
time: 46 us; the launch traced here: 45.1 us
  Pallas kernels  39.1 us (85%)
  local copies, waits for them, and re-layouts  3.5 us (8%)
  between operations  1.29 us (3%)
  other arithmetic  1.25 us (3%)
    pallas_call x1, Pallas kernels, local(): pl.pallas_call(functools.partial(fused_kernel, (heads, blocks, sessions,...  39.1 us
    unnamed x2, local copies, waits for them, and re-layouts  3.5 us
    reduce_min x1, other arithmetic, local(): jnp.min(jnp.where(named, jnp.arange(row_count, dtype=jnp.int32)[None, :],...  1.25 us

profile of v5, /device:TPU:1, one launch (start us, length us, event | category | flops | bytes accessed | tf_op | source)
XLA Modules:
  0.0 45.1 jit_solution(12995056451143439293)
XLA Ops:
  1.3 1.3 %select_reduce_fusion.place_ref = s32[64]{0:T(128)} fusion(s32[32]{0:T(128)} %bitcast.39), kind=kLoop, calls=%fused_computation | loop fusion | flops 6080 | bytes 384 | tf_op jit(solution)/shard_map/reduce_min | solution.py:412
  2.5 39.1 %shard_map.113 = (bf16[768,4096]{1,0:T(8,128)(2,1)S(1)}, bf16[2048,128]{1,0:T(8,128)(2,1)S(1)}) custom-call(s32[1]{0:T(128)S(6)} %copy.24.valid_ref, s32[64]{0:T(128)} %select_reduce_fusion.place_ref, s32[32]{0:T(128)} %bitcast.40, f32[32,768]{1,0:T(8,128)} %bitcast.37, bf16[4,16,32]{2,1,0:T(8,128)(2,1)} %bitcast.38, bf16[768,4096]{1,0:T(8,128)(2,1)} %bitcast.31, ...), custom_call_target="tpu_custom_call" | custom-call | tf_op jit(solution)/shard_map/pallas_call | solution.py:420
  41.6 2.7 %copy.22 = bf16[1,768,4096]{2,1,0:T(8,128)(2,1)} copy(bf16[1,768,4096]{2,1,0:T(8,128)(2,1)S(1)} %bitcast.29) | data formatting | bytes 12582912
  44.3 0.8 %copy.23 = bf16[32,4,2048]{2,1,0:T(4,128)(2,1)} copy(bf16[32,4,2048]{2,1,0:T(4,128)(2,1)S(1)} %bitcast.30) | data formatting | bytes 1048576

commit v6 on v5

--- a/solution.py
+++ b/solution.py
@@ -63,7 +63,7 @@
     out_ref, decoded_ref,
     qb, kb, vb, rates_ref, step_rates_ref, sq, sk, sv, slots, arrived, projected, back, recent, carry_gain, gain_table,
     states, other_states, decays, other_decays,
-    key_gain, block_gain, entry_gain, row_gain, query_gain, floor, mixed, raw,
+    key_gain, block_gain, entry_gain, row_gain, query_gain, floor, mixed,
     load_sem, step_sem, send_sem, recv_sem, pair_send_sem, pair_recv_sem,
 ):
     heads, blocks, sessions, rows_here, steps, (side_z, side_y, side_x) = sizes
@@ -109,12 +109,13 @@
 
     small[0].wait()
 
-    def fill(s, carry):
-        row = place_ref[s]
-        slots[s] = jnp.where(row < rows_here, sq[jnp.minimum(row, rows_here - 1)], jnp.zeros(sq.shape[1:], BF16))
+    def fill(n, carry):
+        for one in range(8):
+            row = place_ref[n * 8 + one]
+            slots[n * 8 + one] = jnp.where(row < rows_here, sq[jnp.minimum(row, rows_here - 1)], jnp.zeros(sq.shape[1:], BF16))
         return carry
 
-    lax.fori_loop(0, sessions, fill, 0)
+    lax.fori_loop(0, sessions // 8, fill, 0)
     arrived[sessions - 1] = slots[me]
 
     pl.semaphore_wait(barrier, sessions)
@@ -299,6 +300,9 @@
 
     def apply_values(lap):
         j, g = place_of(lap)
+        alive = jnp.where(j == 0, live[0], live[1])
+        for n in range(2, blocks):
+            alive = jnp.where(j == n, live[n], alive)
         v4 = vb[block_rows(j), group_cols(g)]
         for one in range(4):
             h = g * 4 + one
@@ -306,27 +310,16 @@
             prefix = jnp.where(first_core, 0.0, entry_gain[j, pl.ds(h, 1), :] * other_states[h])
             entering = (prefix + states[j, h]).astype(BF16)
             for side in range(2):
+                here = slice(side * half, (side + 1) * half)
                 seen = (side + 1) * half
                 weights = mixed[one, :, side * 2 * half:side * 2 * half + seen + half]
-                raw[one, side * half:(side + 1) * half, :] = dot(weights, jnp.concatenate([v[:seen], entering], axis=0))
-
-    def normalize(lap):
-        j, g = place_of(lap)
-        alive = jnp.where(j == 0, live[0], live[1])
-        for n in range(2, blocks):
-            alive = jnp.where(j == n, live[n], alive)
-        for one in range(4):
-            h = g * 4 + one
-            for side in range(2):
-                here = slice(side * half, (side + 1) * half)
-                mix = raw[one, here, :]
+                mix = dot(weights, jnp.concatenate([v[:seen], entering], axis=0))
                 low = jnp.where(iota((half, DH), 1) == h, floor[j, here, :], 0.0)
                 scale = lax.rsqrt(jnp.sum(mix * mix + low, axis=1, keepdims=True)) * alive
                 out_ref[pl.ds(pl.multiple_of(j * BLK + side * half, half), half), pl.ds(pl.multiple_of(h * DH, DH), DH)] = (
                     mix * scale).astype(BF16)
 
     def output_lap(lap, carry):
-        normalize(lap - 2)
         apply_values(lap - 1)
         start_scores(lap)
         return carry
@@ -361,7 +354,6 @@
 
         lax.fori_loop(0, share // 4, project, 0)
 
-    raw[...] = jnp.zeros(raw.shape, F32)
     mixed[...] = jnp.zeros(mixed.shape, BF16)
     decay_copy.wait()
     send_states(pl.multiple_of(core * share, share), share, 0).wait()
@@ -381,19 +373,23 @@
     for n in range(count_a, sessions - 1):
         give_back(n).start()
 
-    lax.fori_loop(EARLY, laps + 2, output_lap, 0)
+    lax.fori_loop(EARLY, laps + 1, output_lap, 0)
 
     wait_all(projected, back, (0, sessions - 1), 2)
 
-    def finish(p, carry):
+    def finish_part(p):
         rows = part_rows(p)
         pieces = [back[session_ref[p * 4 + i]].astype(F32) for i in range(4)]
         reading = carry_gain[rows, :] * jnp.concatenate(pieces, axis=0) + recent[rows, :]
         scale = lax.rsqrt(jnp.mean(reading * reading, axis=1, keepdims=True) + EPSILON)
         decoded_ref[rows, :] = (reading * scale).astype(BF16)
+
+    def finish(p, carry):
+        finish_part(p * 2)
+        finish_part(p * 2 + 1)
         return carry
 
-    lax.fori_loop(0, rows_here // 4, finish, 0)
+    lax.fori_loop(0, rows_here // 8, finish, 0)
 
 
 def local(side, query_rows, key_rows, value_rows, decay_rates, valid_blocks, step_queries, step_keys, step_values, step_rates, row_session):
@@ -433,7 +429,7 @@
             pltpu.VMEM((heads, 8, DH), F32), pltpu.VMEM((heads, 8, DH), F32),
             pltpu.VMEM((blocks, heads, BLK), F32), pltpu.VMEM((blocks, heads, DH), F32), pltpu.VMEM((blocks, heads, DH), F32),
             pltpu.VMEM((blocks, subs, heads, BLK), F32), pltpu.VMEM((blocks, subs, heads, DH), F32),
-            pltpu.VMEM((blocks, BLK, DH), F32), pltpu.VMEM((4, BLK // 2, 5 * BLK // 2), BF16), pltpu.VMEM((4, BLK, DH), F32),
+            pltpu.VMEM((blocks, BLK, DH), F32), pltpu.VMEM((4, BLK // 2, 5 * BLK // 2), BF16),
             dma((3, blocks)), dma((5,)), dma((3,)), dma((3,)), dma((3,)), dma((3,)),
         ],
         compiler_params=pltpu.CompilerParams(collective_id=0, has_side_effects=True, vmem_limit_bytes=48 << 20),

time: 46 us -> 44.8 us (0.974)
  Pallas kernels: 39.1 us -> 38 us
    pallas_call x1, Pallas kernels: 39.1 us -> 38 us  [local(): pl.pallas_call(functools.partial(fused_kernel, (heads, blocks, sessions,...]
where the time goes in v6:
time: 44.8 us; the launch traced here: 44.1 us
  Pallas kernels  38 us (85%)
  local copies, waits for them, and re-layouts  3.5 us (8%)
  between operations  1.29 us (3%)
  other arithmetic  1.25 us (3%)
    pallas_call x1, Pallas kernels, local(): pl.pallas_call(functools.partial(fused_kernel, (heads, blocks, sessions,...  38 us
    unnamed x2, local copies, waits for them, and re-layouts  3.5 us
    reduce_min x1, other arithmetic, local(): jnp.min(jnp.where(named, jnp.arange(row_count, dtype=jnp.int32)[None, :],...  1.25 us

profile of v6, /device:TPU:1, one launch (start us, length us, event | category | flops | bytes accessed | tf_op | source)
XLA Modules:
  0.0 44.1 jit_solution(16725863259942708011)
XLA Ops:
  1.3 1.3 %select_reduce_fusion.place_ref = s32[64]{0:T(128)} fusion(s32[32]{0:T(128)} %bitcast.39), kind=kLoop, calls=%fused_computation | loop fusion | flops 6080 | bytes 384 | tf_op jit(solution)/shard_map/reduce_min | solution.py:408
  2.5 38.0 %shard_map.113 = (bf16[768,4096]{1,0:T(8,128)(2,1)S(1)}, bf16[2048,128]{1,0:T(8,128)(2,1)S(1)}) custom-call(s32[1]{0:T(128)S(6)} %copy.24.valid_ref, s32[64]{0:T(128)} %select_reduce_fusion.place_ref, s32[32]{0:T(128)} %bitcast.40, f32[32,768]{1,0:T(8,128)} %bitcast.37, bf16[4,16,32]{2,1,0:T(8,128)(2,1)} %bitcast.38, bf16[768,4096]{1,0:T(8,128)(2,1)} %bitcast.31, ...), custom_call_target="tpu_custom_call" | custom-call | tf_op jit(solution)/shard_map/pallas_call | solution.py:416
  40.6 2.7 %copy.22 = bf16[1,768,4096]{2,1,0:T(8,128)(2,1)} copy(bf16[1,768,4096]{2,1,0:T(8,128)(2,1)S(1)} %bitcast.29) | data formatting | bytes 12582912
  43.3 0.8 %copy.23 = bf16[32,4,2048]{2,1,0:T(4,128)(2,1)} copy(bf16[32,4,2048]{2,1,0:T(4,128)(2,1)S(1)} %bitcast.30) | data formatting | bytes 1048576

commit v7 on v6

--- a/solution.py
+++ b/solution.py
@@ -16,7 +16,7 @@
 BF16 = jnp.bfloat16
 MESH = pl.DeviceIdType.MESH
 LN2 = math.log(2.0)
-EARLY = 3
+EARLY = 2
 
 
 def dot(a, b, dims=((1,), (0,))):
@@ -276,7 +276,7 @@
         lap = jnp.clip(lap, 0, laps - 1)
         return lax.div(lap, groups), lax.rem(lap, groups)
 
-    def start_scores(lap):
+    def start_scores(lap, twin):
         j, g = place_of(lap)
         rows, cols = block_rows(j), group_cols(g)
         q4, k4 = qb[rows, cols], kb[rows, cols]
@@ -296,9 +296,9 @@
                     latest = jnp.where(causal, piece[:, seen - half:], 0.0)
                     scaled = q[here][b * SUB:(b + 1) * SUB].astype(F32) * query_gain[j, n, pl.ds(h, 1), :]
                     pieces.append(jnp.concatenate(([piece[:, :half]] if side else []) + [latest, scaled], axis=1).astype(BF16))
-                mixed[one, :, side * 2 * half:side * 2 * half + seen + half] = jnp.concatenate(pieces, axis=0)
-
-    def apply_values(lap):
+                mixed[twin * 4 + one, :, side * 2 * half:side * 2 * half + seen + half] = jnp.concatenate(pieces, axis=0)
+
+    def apply_values(lap, twin):
         j, g = place_of(lap)
         alive = jnp.where(j == 0, live[0], live[1])
         for n in range(2, blocks):
@@ -312,7 +312,7 @@
             for side in range(2):
                 here = slice(side * half, (side + 1) * half)
                 seen = (side + 1) * half
-                weights = mixed[one, :, side * 2 * half:side * 2 * half + seen + half]
+                weights = mixed[twin * 4 + one, :, side * 2 * half:side * 2 * half + seen + half]
                 mix = dot(weights, jnp.concatenate([v[:seen], entering], axis=0))
                 low = jnp.where(iota((half, DH), 1) == h, floor[j, here, :], 0.0)
                 scale = lax.rsqrt(jnp.sum(mix * mix + low, axis=1, keepdims=True)) * alive
@@ -320,8 +320,10 @@
                     mix * scale).astype(BF16)
 
     def output_lap(lap, carry):
-        apply_values(lap - 1)
-        start_scores(lap)
+        for twin in range(2):
+            apply_values(2 * lap - 2 + twin, twin)
+        for twin in range(2):
+            start_scores(2 * lap + twin, twin)
         return carry
 
     def project_group(low, high):
@@ -373,7 +375,7 @@
     for n in range(count_a, sessions - 1):
         give_back(n).start()
 
-    lax.fori_loop(EARLY, laps + 1, output_lap, 0)
+    lax.fori_loop(EARLY, laps // 2 + 1, output_lap, 0)
 
     wait_all(projected, back, (0, sessions - 1), 2)
 
@@ -429,7 +431,7 @@
             pltpu.VMEM((heads, 8, DH), F32), pltpu.VMEM((heads, 8, DH), F32),
             pltpu.VMEM((blocks, heads, BLK), F32), pltpu.VMEM((blocks, heads, DH), F32), pltpu.VMEM((blocks, heads, DH), F32),
             pltpu.VMEM((blocks, subs, heads, BLK), F32), pltpu.VMEM((blocks, subs, heads, DH), F32),
-            pltpu.VMEM((blocks, BLK, DH), F32), pltpu.VMEM((4, BLK // 2, 5 * BLK // 2), BF16),
+            pltpu.VMEM((blocks, BLK, DH), F32), pltpu.VMEM((8, BLK // 2, 5 * BLK // 2), BF16),
             dma((3, blocks)), dma((5,)), dma((3,)), dma((3,)), dma((3,)), dma((3,)),
         ],
         compiler_params=pltpu.CompilerParams(collective_id=0, has_side_effects=True, vmem_limit_bytes=48 << 20),

time: 44.8 us -> 44.5 us (level)
  no operation moved by 1% of the time
where the time goes in v7:
time: 44.5 us; the launch traced here: 43.7 us
  Pallas kernels  37.7 us (85%)
  local copies, waits for them, and re-layouts  3.5 us (8%)
  between operations  1.29 us (3%)
  other arithmetic  1.25 us (3%)
    pallas_call x1, Pallas kernels, local(): pl.pallas_call(functools.partial(fused_kernel, (heads, blocks, sessions,...  37.7 us
    unnamed x2, local copies, waits for them, and re-layouts  3.5 us
    reduce_min x1, other arithmetic, local(): jnp.min(jnp.where(named, jnp.arange(row_count, dtype=jnp.int32)[None, :],...  1.25 us

profile of v7, /device:TPU:1, one launch (start us, length us, event | category | flops | bytes accessed | tf_op | source)
XLA Modules:
  0.0 43.7 jit_solution(10121506048669559705)
XLA Ops:
  1.3 1.3 %select_reduce_fusion.place_ref = s32[64]{0:T(128)} fusion(s32[32]{0:T(128)} %bitcast.39), kind=kLoop, calls=%fused_computation | loop fusion | flops 6080 | bytes 384 | tf_op jit(solution)/shard_map/reduce_min | solution.py:410
  2.5 37.7 %shard_map.113 = (bf16[768,4096]{1,0:T(8,128)(2,1)S(1)}, bf16[2048,128]{1,0:T(8,128)(2,1)S(1)}) custom-call(s32[1]{0:T(128)S(6)} %copy.24.valid_ref, s32[64]{0:T(128)} %select_reduce_fusion.place_ref, s32[32]{0:T(128)} %bitcast.40, f32[32,768]{1,0:T(8,128)} %bitcast.37, bf16[4,16,32]{2,1,0:T(8,128)(2,1)} %bitcast.38, bf16[768,4096]{1,0:T(8,128)(2,1)} %bitcast.31, ...), custom_call_target="tpu_custom_call" | custom-call | tf_op jit(solution)/shard_map/pallas_call | solution.py:418
  40.2 2.7 %copy.22 = bf16[1,768,4096]{2,1,0:T(8,128)(2,1)} copy(bf16[1,768,4096]{2,1,0:T(8,128)(2,1)S(1)} %bitcast.29) | data formatting | bytes 12582912
  42.9 0.8 %copy.23 = bf16[32,4,2048]{2,1,0:T(4,128)(2,1)} copy(bf16[32,4,2048]{2,1,0:T(4,128)(2,1)S(1)} %bitcast.30) | data formatting | bytes 1048576
